TPU v7x, 256 devices: a whole 4x4x8 slice. The times are simulated.
256 devices in a mesh: patch: 16 (over y, z_hi, core), tp: 16 (over z_lo, x).
Axes of the slice: x: 4, y: 4, z: 8 (z_hi: 2, z_lo: 4; z = z_hi * 4 + z_lo), core: 2. Of those that a mesh axis runs over, the one named last changes fastest.
Arguments:
- latent: bfloat16 [4096, 3072], P('patch', 'tp'), may hold values from -25 to 25, as said below
- modulation: float32 [2, 3, 3072], replicated, may hold values from -4 to 4
- stale_kv: bfloat16 [2, 4096, 2048], P(None, 'patch', 'tp'), may hold values from -40 to 40
- w_qkv: bfloat16 [3072, 3, 2048], P(('patch', 'tp')), may hold values from -0.109375 to 0.109375
- w_out: bfloat16 [3072, 2048], P('tp', 'patch'), may hold values from -0.25 to 0.25
- q_gain: float32 [128], replicated, may hold values from 0.7 to 3
- k_gain: float32 [128], replicated, may hold values from 0.7 to 3
Outputs:
- latent_out: bfloat16 [4096, 3072], P('patch', 'tp')
- next_kv: bfloat16 [2, 4096, 2048], P(None, 'patch', 'tp')
Inputs may be any that keep to these rules, and one draw needn't show every extreme that they name: latent tokens of varying scale.
All inputs are finite; a program needn't handle non-finite values.
Results may differ from a plain program's by a relative error of at most 0.03.
Values may be sent and summed in bfloat16 or wider, within the bound.
No kernel may reach another device: no remote copies, remote signals or barrier semaphores. Data moves between devices by JAX's collectives and lax.ppermute only.
A program may use at most 64 MiB of HBM per device.

v0:
```python
import functools

import jax
import jax.numpy as jnp
from jax import lax
from jax.experimental import pallas as pl
from jax.experimental.pallas import tpu as pltpu
from jax.sharding import PartitionSpec as P

NY, NH, NC = 4, 2, 2
NL, NX = 4, 4
N_TP = NL * NX
N_PATCH = NY * NH * NC
STEPS = 2
EPS = 1e-06
BF = jnp.bfloat16
F32 = jnp.float32
LOG2E = 1.4426950408889634


def shift(array, axis, amount):
    if axis in ("l", "x"):
        pairs = []
        for l in range(NL):
            for x in range(NX):
                to = ((l + amount) % NL, x) if axis == "l" else (l, (x + amount) % NX)
                pairs.append((l * NX + x, to[0] * NX + to[1]))
        return lax.ppermute(array, "tp", pairs)
    pairs = []
    for y in range(NY):
        for h in range(NH):
            for c in range(NC):
                to = {
                    "y": ((y + amount) % NY, h, c),
                    "h": (y, (h + amount) % NH, c),
                    "c": (y, h, (c + amount) % NC),
                }[axis]
                pairs.append(((y * NH + h) * NC + c, (to[0] * NH + to[1]) * NC + to[2]))
    return lax.ppermute(array, "patch", pairs)


def shifts(array, axis, count):
    return [shift(array, axis, k) for k in range(1, count)]


def sync(*trees):
    leaves, kind = jax.tree.flatten(trees)
    return jax.tree.unflatten(kind, lax.optimization_barrier(tuple(leaves)))


def call(body, outs, inputs, scratch, cost, room, name):
    vector = pl.BlockSpec(memory_space=pltpu.VMEM)
    return pl.pallas_call(
        body,
        out_shape=outs,
        in_specs=[pl.BlockSpec(memory_space=pltpu.SMEM)] + [vector] * (len(inputs) - 1),
        out_specs=[vector] * len(outs),
        scratch_shapes=scratch,
        compiler_params=pltpu.CompilerParams(vmem_limit_bytes=room << 20),
        cost_estimate=pl.CostEstimate(flops=1 << 20, bytes_accessed=cost << 20, transcendentals=0),
        name=name,
    )(*inputs)


def dot(a, b, dims):
    return lax.dot_general(a, b, (dims, ((), ())), preferred_element_type=F32)


def blocks(refs, table):
    return [(ref, i, first + i) for ref, first in zip(refs, table) for i in range(ref.shape[0])]


def tp_of(ids, n):
    l, x = ids[1] // NX, ids[1] % NX
    return ((l + NL - n % NL) % NL) * NX + (x + NX - n // NL) % NX


def patch_of(ids, n):
    patch = ids[0]
    y, h, c = patch // (NH * NC), (patch // NC) % NH, patch % NC
    ky, kh, kc = (n // NH) % NY, n % NH, n // (NH * NY)
    return (((y + NY - ky) % NY) * NH + (h + kh) % NH) * NC + (c + kc) % NC


def norm_body(step, ids, mod, *refs):
    groups, (normed, rows) = refs[:NX], refs[NX:]
    feat, tok = normed.shape[1:]
    total = feat * N_TP
    places = blocks(groups, [NL * k for k in range(NX)])
    rows[...] = jnp.zeros_like(rows)
    for n in range(N_TP):
        t = tp_of(ids, n)
        rows[n : n + 1, 0:feat] = mod[pl.ds((step * 3 + 1) * N_TP + t, 1), :] + 1.0
        rows[n + 16 : n + 17, 0:feat] = mod[pl.ds(step * 3 * N_TP + t, 1), :]
    cols = jnp.transpose(rows[...])
    mean = jnp.zeros((1, tok), F32)
    for ref, i, n in places:
        mean += jnp.sum(ref[i].astype(F32), axis=0, keepdims=True)
    mean = mean / total
    spread = jnp.zeros((1, tok), F32)
    for ref, i, n in places:
        centre = ref[i].astype(F32) - mean
        spread += jnp.sum(centre * centre, axis=0, keepdims=True)
    rstd = lax.rsqrt(spread / total + EPS)
    for ref, i, n in places:
        block = (ref[i].astype(F32) - mean) * rstd
        block = block * cols[0:feat, n : n + 1] + cols[0:feat, n + 16 : n + 17]
        normed[tp_of(ids, n)] = block.astype(BF)


def qkv_body(table, ids, normed, qg, kg, *refs):
    weights, (kv_out, near) = refs[: len(table)], refs[len(table) :]
    tok, size = normed.shape[2], qg.shape[-1]
    qkv = jnp.zeros((tok, 3 * size), F32)
    for ref, i, n in blocks(weights, table):
        qkv += dot(normed[patch_of(ids, n)], ref[i, :, 0 : 3 * size], ((0,), (0,)))
    for n, gain in enumerate((qg, kg)):
        one = qkv[:, n * size : (n + 1) * size]
        scale = lax.rsqrt(jnp.mean(one * one, axis=-1, keepdims=True) + EPS)
        near[n * tok : (n + 1) * tok] = (one * scale * gain[...]).astype(BF)
    near[2 * tok :] = qkv[:, 2 * size :].astype(BF)
    kv_out[...] = near[tok:]


def attend_body(ids, near, past, out, scores):
    tok, size = near.shape[0] // 3, near.shape[1]

    def block(n, rows):
        own = near[tok + rows.start : tok + rows.stop]
        return jnp.where(ids[0] == n, own, past[n, rows])

    q = near[0:tok]
    top = jnp.full((1, tok), -jnp.inf, F32)
    for n in range(N_PATCH):
        part = dot(block(n, slice(0, tok)), q, ((1,), (1,)))
        scores[n] = part
        top = jnp.maximum(top, jnp.max(part, axis=0, keepdims=True))
    inv = LOG2E / size**0.5
    total = jnp.zeros((1, tok), F32)
    mixed = jnp.zeros((size, tok), F32)
    for n in range(N_PATCH):
        p = jnp.exp2((scores[n] - top) * inv)
        total += jnp.sum(p, axis=0, keepdims=True)
        mixed += dot(block(n, slice(tok, 2 * tok)), p.astype(BF), ((0,), (0,)))
    out[...] = (mixed / total).astype(BF)


def arrange_body(table, ids, *refs):
    weights, out = refs[:-1], refs[-1]
    size = out.shape[1] // NL
    feat = out.shape[0] // NX
    l, x = ids[1] // NX, ids[1] % NX
    for ref, i, n in blocks(weights, table):
        patch = patch_of(ids, n)
        k = (patch % NX + NX - x) % NX
        kl = (l + NL - patch // NX) % NL
        rows = pl.ds(pl.multiple_of(k * feat, feat), feat)
        lanes = pl.ds(pl.multiple_of(kl * size, size), size)
        out[rows, lanes] = ref[i, :, 3 * size :]


def partial_body(ids, weights, *refs):
    attn, outs, mixed = refs[:NL], refs[NL:-1], refs[-1]
    size, feat = attn[0].shape[0], outs[0].shape[0]
    for n, part in enumerate(attn):
        mixed[n * size : (n + 1) * size] = part[...]
    acc = dot(weights[...], mixed[...], ((1,), (0,)))
    for n, out in enumerate(outs):
        out[...] = acc[n * feat : (n + 1) * feat].astype(out.dtype)


def update_body(step, ids, mod, x, own, *refs):
    came, (out, rows) = refs[:-2], refs[-2:]
    feat = x.shape[0]
    rows[...] = jnp.zeros_like(rows)
    rows[0:1, 0:feat] = mod[pl.ds((step * 3 + 2) * N_TP + ids[1], 1), :]
    gate = jnp.transpose(rows[...])[0:feat, 0:1]
    acc = own[...]
    for part in came:
        acc += part[...].astype(F32)
    out[...] = (x[...].astype(F32) + gate * acc).astype(BF)


def swap(array):
    pairs = []
    for y in range(NY):
        for m in range(NH * NC):
            for l in range(NL):
                for x in range(NX):
                    here = (y * NX + m) * N_TP + l * NX + x
                    pairs.append((here, (y * NX + x) * N_TP + l * NX + m))
    return lax.ppermute(array, ("patch", "tp"), pairs)


def on_device(latent, modulation, stale_kv, w_qkv, w_out, q_gain, k_gain):
    tok, feat = latent.shape
    size = q_gain.shape[0]
    ids = jnp.stack([lax.axis_index("patch"), lax.axis_index("tp")]).astype(jnp.int32)
    mod = modulation.reshape(STEPS * 3 * N_TP, feat)
    qg, kg = q_gain.reshape(1, size), k_gain.reshape(1, size)
    x = latent.T

    def shape(*dims):
        return jax.ShapeDtypeStruct(dims, BF)

    def norm(step, groups):
        return call(
            functools.partial(norm_body, step),
            [shape(N_TP, feat, tok)],
            [ids, mod, *groups],
            [pltpu.VMEM((128, 256), F32)],
            4,
            8,
            "norm",
        )[0]

    rows_dev = w_qkv.shape[0]
    sent = w_qkv.reshape(rows_dev, 3, N_TP, size).transpose(2, 1, 0, 3).reshape(N_TP, 3 * rows_dev, size)
    cache = stale_kv.reshape(2 * tok, size)
    w_mine = lax.all_to_all(sent, "tp", 0, 0)
    x_l = shifts(x, "l", NL)
    cache_all = lax.all_gather(cache, "patch")
    w_back = swap(w_out)
    x, x_l, w_back, w_mine, ids, mod = sync(x, x_l, w_back, w_mine, ids, mod)
    w_mine = w_mine.reshape(N_TP, 3, rows_dev, size).transpose(0, 2, 1, 3).reshape(N_TP * rows_dev, 3 * size)
    w_mine = jnp.concatenate([w_mine, w_back], axis=1)
    w_h = shift(w_mine, "h", 1)
    x_four = jnp.stack([x] + x_l)
    x_up, x_down = shift(x_four, "x", 1), shift(x_four, "x", 3)
    w_h, x_up, x_down = sync(w_h, x_up, x_down)
    w_pair = jnp.stack([w_mine, w_h])
    w_quad = [w_pair] + shifts(w_pair, "y", NY)
    x_far = shift(x_four, "x", 2)
    w_c = [shift(piece, "c", 1) for piece in w_quad]
    normed = norm(0, [x_four, x_up, x_far, x_down])
    w_c, w_quad, normed = sync(w_c, w_quad, normed)
    past = cache_all
    weights, w_table = w_quad + w_c, [NH * k for k in range(NC * NY)]
    for step in range(STEPS):
        last = step + 1 == STEPS
        kv, near = call(
            functools.partial(qkv_body, w_table),
            [shape(2 * tok, size), shape(3 * tok, size)],
            [ids, normed, qg, kg, *weights],
            [],
            16,
            8,
            "qkv",
        )
        if not last:
            kv_all = lax.all_gather(kv, "patch")
        (attn,) = call(
            attend_body,
            [shape(size, tok)],
            [ids, near, past],
            [pltpu.VMEM((N_PATCH, tok, tok), F32)],
            8,
            12,
            "attend",
        )
        if not step:
            (w_all,) = call(
                functools.partial(arrange_body, w_table),
                [shape(NX * feat, NL * size)],
                [ids, *weights],
                [],
                3,
                8,
                "arrange",
            )
        came = shifts(attn, "l", NL)
        came, w_all = sync(came, w_all)
        own, *parts = call(
            partial_body,
            [jax.ShapeDtypeStruct((feat, tok), F32)] + [shape(feat, tok)] * (NX - 1),
            [ids, w_all, attn, *came],
            [pltpu.VMEM((NL * size, tok), BF)],
            2,
            8,
            "partial",
        )
        sums = [shift(part, "x", k + 1) for k, part in enumerate(parts)]
        (x,) = call(
            functools.partial(update_body, step),
            [shape(feat, tok)],
            [ids, mod, x, own, *sums],
            [pltpu.VMEM((128, 256), F32)],
            1,
            4,
            "update",
        )
        if last:
            break
        x_l = shifts(x, "l", NL)
        x_four = jnp.stack([x] + x_l)
        groups = [x_four] + shifts(x_four, "x", NX)
        normed = norm(step + 1, groups)
        past = kv_all
    return x.T, kv.reshape(2, tok, size)


def solution(mesh):
    in_specs = (
        P("patch", "tp"),
        P(),
        P(None, "patch", "tp"),
        P(("patch", "tp"), None, None),
        P("tp", "patch"),
        P(),
        P(),
    )
    out_specs = (P("patch", "tp"), P(None, "patch", "tp"))
    return jax.shard_map(on_device, mesh=mesh, in_specs=in_specs, out_specs=out_specs, check_vma=False)
```

profile of v0, /device:TPU:6, one launch (start us, length us, event | category | flops | bytes accessed | tf_op | source)
XLA Modules:
  0.0 178.7 jit_solution(2734272994263995024)
XLA Ops:
  9.7 8.9 %all-to-all-start = ((bf16[16,36,128]{2,1,0:T(8,128)(2,1)}), bf16[16,36,128]{2,1,0:T(8,128)(2,1)S(1)}, u32[]{:S(2)}, u32[]{:S(2)}) async-start(bf16[16,36,128]{2,1,0:T(8,128)(2,1)} %copy.14), calls=%async_computation | async-start | bytes 327680 | tf_op jit(solution)/shard_map/all_to_all | solution.py:220
  20.2 2.4 %collective-permute-start.1 = (bf16[192,256]{1,0:T(8,128)(2,1)}, bf16[192,256]{1,0:T(8,128)(2,1)S(1)}, u32[]{:S(2)}, u32[]{:S(2)}) collective-permute-start(bf16[192,256]{1,0:T(8,128)(2,1)} %bitcast.32), channel_id=1, source_target_pairs={{0,8},{1,9},{2,10},{3,11},{4,12},{5,13},{6,14},{7,15},{8,0},{9,1},... | collective-permute-start | bytes 294920 | tf_op jit(solution)/shard_map/ppermute | solution.py:28
  24.0 4.4 %collective-permute-start.3 = (bf16[192,128]{1,0:T(8,128)(2,1)}, bf16[192,128]{1,0:T(8,128)(2,1)S(1)}, u32[]{:S(2)}, u32[]{:S(2)}) collective-permute-start(bf16[192,128]{1,0:T(8,128)(2,1)} %param.11), channel_id=1, source_target_pairs={{0,0},{1,16},{2,32},{3,48},{4,4},{5,20},{6,36},{7,52},{8,8},{9,24}... | collective-permute-start | bytes 147464 | tf_op jit(solution)/shard_map/ppermute | solution.py:192
  29.5 6.6 %collective-permute-done.3 = bf16[192,128]{1,0:T(8,128)(2,1)S(1)} collective-permute-done((bf16[192,128]{1,0:T(8,128)(2,1)}, bf16[192,128]{1,0:T(8,128)(2,1)S(1)}, u32[]{:S(2)}, u32[]{:S(2)}) %collective-permute-start.3) | collective-permute-done | bytes 49184 | tf_op jit(solution)/shard_map/ppermute | solution.py:192
  39.5 4.0 %collective-permute-start.4 = (bf16[192,512]{1,0:T(8,128)(2,1)S(1)}, bf16[192,512]{1,0:T(8,128)(2,1)S(1)}, u32[]{:S(2)}, u32[]{:S(2)}) collective-permute-start(bf16[192,512]{1,0:T(8,128)(2,1)S(1)} %constant_dynamic-update-slice_fusion), channel_id=1, source_target_pairs={{0,32},{16,48},{32,0},{48,16},{64,96},{80,112},{96,64},{112,80},{1... | collective-permute-start | bytes 589832 | tf_op jit(solution)/shard_map/ppermute | solution.py:39
  43.5 5.8 %collective-permute-done.4 = bf16[192,512]{1,0:T(8,128)(2,1)S(1)} collective-permute-done((bf16[192,512]{1,0:T(8,128)(2,1)S(1)}, bf16[192,512]{1,0:T(8,128)(2,1)S(1)}, u32[]{:S(2)}, u32[]{:S(2)}) %collective-permute-start.4) | collective-permute-done | bytes 196640 | tf_op jit(solution)/shard_map/ppermute | solution.py:39
  49.3 3.2 %collective-permute-start.10 = (bf16[2,192,512]{2,1,0:T(8,128)(2,1)S(1)}, bf16[2,192,512]{2,1,0:T(8,128)(2,1)S(1)}, u32[]{:S(2)}, u32[]{:S(2)}) collective-permute-start(bf16[2,192,512]{2,1,0:T(8,128)(2,1)S(1)} %pad_maximum_fusion.1.refs_0_), channel_id=1, source_target_pairs={{0,128},{16,144},{32,160},{48,176},{64,192},{80,208},{96,224},{112... | collective-permute-start | bytes 1179656 | tf_op jit(solution)/shard_map/ppermute | solution.py:39
  56.0 8.4 %collective-permute-done.10.refs_2_ = bf16[2,192,512]{2,1,0:T(8,128)(2,1)S(1)} collective-permute-done((bf16[2,192,512]{2,1,0:T(8,128)(2,1)S(1)}, bf16[2,192,512]{2,1,0:T(8,128)(2,1)S(1)}, u32[]{:S(2)}, u32[]{:S(2)}) %collective-permute-start.10) | collective-permute-done | bytes 393248 | tf_op jit(solution)/shard_map/ppermute | solution.py:39
  64.4 6.3 %collective-permute-done.12.refs_3_ = bf16[2,192,512]{2,1,0:T(8,128)(2,1)S(1)} collective-permute-done((bf16[2,192,512]{2,1,0:T(8,128)(2,1)S(1)}, bf16[2,192,512]{2,1,0:T(8,128)(2,1)S(1)}, u32[]{:S(2)}, u32[]{:S(2)}) %collective-permute-start.12) | collective-permute-done | bytes 393248 | tf_op jit(solution)/shard_map/ppermute | solution.py:39
  71.2 2.2 %norm.2.normed = bf16[16,192,256]{2,1,0:T(8,128)(2,1)S(1)} custom-call(s32[2]{0:T(128)S(1)} %pad_add_fusion.ids, f32[96,192]{1,0:T(8,128)S(1)} %reshape.30.mod, bf16[4,192,256]{2,1,0:T(8,128)(2,1)S(1)} %pad_maximum_fusion.refs_0_, bf16[4,192,256]{2,1,0:T(8,128)(2,1)S(1)} %collective-permute-done.5.refs_1_, ...), custom_call_target="tpu_custom_call" | custom-call | flops 1048576 | bytes 4194304 | tf_op jit(solution)/shard_map/norm/pallas_call | solution.py:53
  73.5 2.7 %qkv.2 = (bf16[512,128]{1,0:T(8,128)(2,1)}, bf16[768,128]{1,0:T(8,128)(2,1)S(1)}) custom-call(s32[2]{0:T(128)S(1)} %pad_add_fusion.ids, bf16[16,192,256]{2,1,0:T(8,128)(2,1)S(1)} %norm.2.normed, f32[1,128]{1,0:T(1,128)S(1)} %bitcast.36, f32[1,128]{1,0:T(1,128)S(1)} %bitcast.38, bf16[2,192,512]{2,1,0:T(8,128)(2,1)S(1)} %pad_maximum_fusion.1.refs_0_, ...), custom_call_target="tpu_custom_call" | custom-call | flops 1048576 | bytes 16777216 | tf_op jit(solution)/shard_map/qkv/pallas_call | solution.py:53
  76.2 4.3 %all-gather.4.cloned.1.call-done.past = bf16[16,512,128]{2,1,0:T(8,128)(2,1)} async-done(((bf16[1,512,128]{2,1,0:T(8,128)(2,1)}), bf16[16,512,128]{2,1,0:T(8,128)(2,1)}) %all-gather.4.cloned.1.call-update) | async-done | bytes 2097168 | tf_op jit(solution)/shard_map/all_gather | solution.py:222
  82.2 2.4 %attend.2.refs_0_ = bf16[128,256]{1,0:T(8,128)(2,1)S(1)} custom-call(s32[2]{0:T(128)S(1)} %pad_add_fusion.ids, bf16[768,128]{1,0:T(8,128)(2,1)S(1)} %get-tuple-element.62.near, bf16[16,512,128]{2,1,0:T(8,128)(2,1)S(1)} %copy-done.5), custom_call_target="tpu_custom_call" | custom-call | flops 1048576 | bytes 8388608 | tf_op jit(solution)/shard_map/attend/pallas_call | solution.py:53
  84.6 3.2 %collective-permute-start.15 = (bf16[128,256]{1,0:T(8,128)(2,1)S(1)}, bf16[128,256]{1,0:T(8,128)(2,1)S(1)}, u32[]{:S(2)}, u32[]{:S(2)}) collective-permute-start(bf16[128,256]{1,0:T(8,128)(2,1)S(1)} %attend.2.refs_0_), channel_id=1, source_target_pairs={{0,4},{1,5},{2,6},{3,7},{4,8},{5,9},{6,10},{7,11},{8,12},{9,13},{1... | collective-permute-start | bytes 196616 | tf_op jit(solution)/shard_map/ppermute | solution.py:28
  89.3 2.8 %collective-permute-start.17 = (bf16[128,256]{1,0:T(8,128)(2,1)S(1)}, bf16[128,256]{1,0:T(8,128)(2,1)S(1)}, u32[]{:S(2)}, u32[]{:S(2)}) collective-permute-start(bf16[128,256]{1,0:T(8,128)(2,1)S(1)} %attend.2.refs_0_), channel_id=1, source_target_pairs={{0,12},{1,13},{2,14},{3,15},{4,0},{5,1},{6,2},{7,3},{8,4},{9,5},{1... | collective-permute-start | bytes 196616 | tf_op jit(solution)/shard_map/ppermute | solution.py:28
  95.1 3.0 %collective-permute-start.18 = (bf16[192,256]{1,0:T(8,128)(2,1)S(1)}, bf16[192,256]{1,0:T(8,128)(2,1)S(1)}, u32[]{:S(2)}, u32[]{:S(2)}) collective-permute-start(bf16[192,256]{1,0:T(8,128)(2,1)S(1)} %get-tuple-element.68), channel_id=1, source_target_pairs={{0,1},{1,2},{2,3},{3,0},{4,5},{5,6},{6,7},{7,4},{8,9},{9,10},{10,1... | collective-permute-start | bytes 294920 | tf_op jit(solution)/shard_map/ppermute | solution.py:28
  99.0 2.3 %collective-permute-done.18.refs_0_ = bf16[192,256]{1,0:T(8,128)(2,1)S(1)} collective-permute-done((bf16[192,256]{1,0:T(8,128)(2,1)S(1)}, bf16[192,256]{1,0:T(8,128)(2,1)S(1)}, u32[]{:S(2)}, u32[]{:S(2)}) %collective-permute-start.18) | collective-permute-done | bytes 98336 | tf_op jit(solution)/shard_map/ppermute | solution.py:28
  101.3 3.0 %collective-permute-done.19.refs_1_ = bf16[192,256]{1,0:T(8,128)(2,1)S(1)} collective-permute-done((bf16[192,256]{1,0:T(8,128)(2,1)S(1)}, bf16[192,256]{1,0:T(8,128)(2,1)S(1)}, u32[]{:S(2)}, u32[]{:S(2)}) %collective-permute-start.19) | collective-permute-done | bytes 98336 | tf_op jit(solution)/shard_map/ppermute | solution.py:28
  107.7 2.2 %collective-permute-start.22 = (bf16[192,256]{1,0:T(8,128)(2,1)S(1)}, bf16[192,256]{1,0:T(8,128)(2,1)S(1)}, u32[]{:S(2)}, u32[]{:S(2)}) collective-permute-start(bf16[192,256]{1,0:T(8,128)(2,1)S(1)} %update.2.x), channel_id=1, source_target_pairs={{0,8},{1,9},{2,10},{3,11},{4,12},{5,13},{6,14},{7,15},{8,0},{9,1},... | collective-permute-start | bytes 294920 | tf_op jit(solution)/shard_map/ppermute | solution.py:28
  110.1 3.2 %collective-permute-done.21 = bf16[192,256]{1,0:T(8,128)(2,1)S(1)} collective-permute-done((bf16[192,256]{1,0:T(8,128)(2,1)S(1)}, bf16[192,256]{1,0:T(8,128)(2,1)S(1)}, u32[]{:S(2)}, u32[]{:S(2)}) %collective-permute-start.21) | collective-permute-done | bytes 98336 | tf_op jit(solution)/shard_map/ppermute | solution.py:28
  113.3 2.9 %collective-permute-done.22 = bf16[192,256]{1,0:T(8,128)(2,1)S(1)} collective-permute-done((bf16[192,256]{1,0:T(8,128)(2,1)S(1)}, bf16[192,256]{1,0:T(8,128)(2,1)S(1)}, u32[]{:S(2)}, u32[]{:S(2)}) %collective-permute-start.22) | collective-permute-done | bytes 98336 | tf_op jit(solution)/shard_map/ppermute | solution.py:28
  119.0 9.5 %collective-permute-done.24.refs_1_ = bf16[4,192,256]{2,1,0:T(8,128)(2,1)S(1)} collective-permute-done((bf16[4,192,256]{2,1,0:T(8,128)(2,1)S(1)}, bf16[4,192,256]{2,1,0:T(8,128)(2,1)S(1)}, u32[]{:S(2)}, u32[]{:S(2)}) %collective-permute-start.24) | collective-permute-done | bytes 393248 | tf_op jit(solution)/shard_map/ppermute | solution.py:28
  128.5 2.2 %collective-permute-done.25.refs_2_ = bf16[4,192,256]{2,1,0:T(8,128)(2,1)S(1)} collective-permute-done((bf16[4,192,256]{2,1,0:T(8,128)(2,1)S(1)}, bf16[4,192,256]{2,1,0:T(8,128)(2,1)S(1)}, u32[]{:S(2)}, u32[]{:S(2)}) %collective-permute-start.25) | collective-permute-done | bytes 393248 | tf_op jit(solution)/shard_map/ppermute | solution.py:28
  130.8 6.3 %collective-permute-done.26.refs_3_ = bf16[4,192,256]{2,1,0:T(8,128)(2,1)S(1)} collective-permute-done((bf16[4,192,256]{2,1,0:T(8,128)(2,1)S(1)}, bf16[4,192,256]{2,1,0:T(8,128)(2,1)S(1)}, u32[]{:S(2)}, u32[]{:S(2)}) %collective-permute-start.26) | collective-permute-done | bytes 393248 | tf_op jit(solution)/shard_map/ppermute | solution.py:28
  137.0 2.2 %norm.3.normed = bf16[16,192,256]{2,1,0:T(8,128)(2,1)S(1)} custom-call(s32[2]{0:T(128)S(1)} %pad_add_fusion.ids, f32[96,192]{1,0:T(8,128)S(1)} %copy-done.3, bf16[4,192,256]{2,1,0:T(8,128)(2,1)S(1)} %pad_maximum_fusion.2.refs_0_, bf16[4,192,256]{2,1,0:T(8,128)(2,1)S(1)} %collective-permute-done.24.refs_1_, ...), custom_call_target="tpu_custom_call" | custom-call | flops 1048576 | bytes 4194304 | tf_op jit(solution)/shard_map/norm/pallas_call | solution.py:53
  139.3 2.7 %qkv.3 = (bf16[512,128]{1,0:T(8,128)(2,1)}, bf16[768,128]{1,0:T(8,128)(2,1)S(1)}) custom-call(s32[2]{0:T(128)S(1)} %pad_add_fusion.ids, bf16[16,192,256]{2,1,0:T(8,128)(2,1)S(1)} %norm.3.normed, f32[1,128]{1,0:T(1,128)S(1)} %bitcast.37, f32[1,128]{1,0:T(1,128)S(1)} %bitcast.39, bf16[2,192,512]{2,1,0:T(8,128)(2,1)S(1)} %pad_maximum_fusion.1.refs_0_, ...), custom_call_target="tpu_custom_call" | custom-call | flops 1048576 | bytes 16777216 | tf_op jit(solution)/shard_map/qkv/pallas_call | solution.py:53
  142.6 3.2 %all-gather.6.cloned.1.call-done = bf16[8192,128]{1,0:T(8,128)(2,1)} async-done(((bf16[512,128]{1,0:T(8,128)(2,1)}), bf16[8192,128]{1,0:T(8,128)(2,1)}) %all-gather.6.cloned.1.call-update) | async-done | bytes 2097168 | tf_op jit(solution)/shard_map/all_gather | solution.py:251
  148.4 2.4 %attend.3.refs_0_ = bf16[128,256]{1,0:T(8,128)(2,1)S(1)} custom-call(s32[2]{0:T(128)S(1)} %pad_add_fusion.ids, bf16[768,128]{1,0:T(8,128)(2,1)S(1)} %copy-done.11, bf16[16,512,128]{2,1,0:T(8,128)(2,1)S(1)} %bitcast.29), custom_call_target="tpu_custom_call" | custom-call | flops 1048576 | bytes 8388608 | tf_op jit(solution)/shard_map/attend/pallas_call | solution.py:53
  151.5 3.2 %collective-permute-start.29 = (bf16[128,256]{1,0:T(8,128)(2,1)S(1)}, bf16[128,256]{1,0:T(8,128)(2,1)S(1)}, u32[]{:S(2)}, u32[]{:S(2)}) collective-permute-start(bf16[128,256]{1,0:T(8,128)(2,1)S(1)} %attend.3.refs_0_), channel_id=1, source_target_pairs={{0,12},{1,13},{2,14},{3,15},{4,0},{5,1},{6,2},{7,3},{8,4},{9,5},{1... | collective-permute-start | bytes 196616 | tf_op jit(solution)/shard_map/ppermute | solution.py:28
  154.7 3.0 %collective-permute-done.27.refs_1_ = bf16[128,256]{1,0:T(8,128)(2,1)S(1)} collective-permute-done((bf16[128,256]{1,0:T(8,128)(2,1)S(1)}, bf16[128,256]{1,0:T(8,128)(2,1)S(1)}, u32[]{:S(2)}, u32[]{:S(2)}) %collective-permute-start.27) | collective-permute-done | bytes 65568 | tf_op jit(solution)/shard_map/ppermute | solution.py:28
  161.4 2.4 %collective-permute-start.31 = (bf16[192,256]{1,0:T(8,128)(2,1)S(1)}, bf16[192,256]{1,0:T(8,128)(2,1)S(1)}, u32[]{:S(2)}, u32[]{:S(2)}) collective-permute-start(bf16[192,256]{1,0:T(8,128)(2,1)S(1)} %get-tuple-element.79), channel_id=1, source_target_pairs={{0,2},{1,3},{2,0},{3,1},{4,6},{5,7},{6,4},{7,5},{8,10},{9,11},{10,... | collective-permute-start | bytes 294920 | tf_op jit(solution)/shard_map/ppermute | solution.py:28
  165.4 2.4 %collective-permute-done.31.refs_1_ = bf16[192,256]{1,0:T(8,128)(2,1)S(1)} collective-permute-done((bf16[192,256]{1,0:T(8,128)(2,1)S(1)}, bf16[192,256]{1,0:T(8,128)(2,1)S(1)}, u32[]{:S(2)}, u32[]{:S(2)}) %collective-permute-start.31) | collective-permute-done | bytes 98336 | tf_op jit(solution)/shard_map/ppermute | solution.py:28
  (94 shorter events, 40.8 us)
Async XLA Ops:
  7.2 73.4 %all-gather.4.cloned.1.call-start = ((), (), s32[]{:S(2)}) async-start(), calls=%async_computation.1 | async-start | bytes 2228224 | tf_op jit(solution)/shard_map/all_gather | solution.py:222
  9.7 26.5 %all-to-all-start = ((bf16[16,36,128]{2,1,0:T(8,128)(2,1)}), bf16[16,36,128]{2,1,0:T(8,128)(2,1)S(1)}, u32[]{:S(2)}, u32[]{:S(2)}) async-start(bf16[16,36,128]{2,1,0:T(8,128)(2,1)} %copy.14), calls=%async_computation | async-start | bytes 327680 | tf_op jit(solution)/shard_map/all_to_all | solution.py:220
  18.6 127.3 %all-gather.6.cloned.1.call-start = ((), (), s32[]{:S(2)}) async-start(), calls=%async_computation.2 | async-start | bytes 2228224 | tf_op jit(solution)/shard_map/all_gather | solution.py:251
  18.6 17.6 %collective-permute-start = (bf16[192,256]{1,0:T(8,128)(2,1)}, bf16[192,256]{1,0:T(8,128)(2,1)S(1)}, u32[]{:S(2)}, u32[]{:S(2)}) collective-permute-start(bf16[192,256]{1,0:T(8,128)(2,1)} %bitcast.31), channel_id=1, source_target_pairs={{0,4},{1,5},{2,6},{3,7},{4,8},{5,9},{6,10},{7,11},{8,12},{9,13},{1... | collective-permute-start | bytes 294920 | tf_op jit(solution)/shard_map/ppermute | solution.py:28
  20.2 16.0 %collective-permute-start.1 = (bf16[192,256]{1,0:T(8,128)(2,1)}, bf16[192,256]{1,0:T(8,128)(2,1)S(1)}, u32[]{:S(2)}, u32[]{:S(2)}) collective-permute-start(bf16[192,256]{1,0:T(8,128)(2,1)} %bitcast.32), channel_id=1, source_target_pairs={{0,8},{1,9},{2,10},{3,11},{4,12},{5,13},{6,14},{7,15},{8,0},{9,1},... | collective-permute-start | bytes 294920 | tf_op jit(solution)/shard_map/ppermute | solution.py:28
  22.5 13.7 %collective-permute-start.2 = (bf16[192,256]{1,0:T(8,128)(2,1)}, bf16[192,256]{1,0:T(8,128)(2,1)S(1)}, u32[]{:S(2)}, u32[]{:S(2)}) collective-permute-start(bf16[192,256]{1,0:T(8,128)(2,1)} %bitcast.33), channel_id=1, source_target_pairs={{0,12},{1,13},{2,14},{3,15},{4,0},{5,1},{6,2},{7,3},{8,4},{9,5},{1... | collective-permute-start | bytes 294920 | tf_op jit(solution)/shard_map/ppermute | solution.py:28
  24.0 12.2 %collective-permute-start.3 = (bf16[192,128]{1,0:T(8,128)(2,1)}, bf16[192,128]{1,0:T(8,128)(2,1)S(1)}, u32[]{:S(2)}, u32[]{:S(2)}) collective-permute-start(bf16[192,128]{1,0:T(8,128)(2,1)} %param.11), channel_id=1, source_target_pairs={{0,0},{1,16},{2,32},{3,48},{4,4},{5,20},{6,36},{7,52},{8,8},{9,24}... | collective-permute-start | bytes 147464 | tf_op jit(solution)/shard_map/ppermute | solution.py:192
  37.2 12.1 %collective-permute-start.5 = (bf16[4,192,256]{2,1,0:T(8,128)(2,1)S(1)}, bf16[4,192,256]{2,1,0:T(8,128)(2,1)S(1)}, u32[]{:S(2)}, u32[]{:S(2)}) collective-permute-start(bf16[4,192,256]{2,1,0:T(8,128)(2,1)S(1)} %pad_maximum_fusion.refs_0_), channel_id=1, source_target_pairs={{0,1},{1,2},{2,3},{3,0},{4,5},{5,6},{6,7},{7,4},{8,9},{9,10},{10,1... | collective-permute-start | bytes 1179656 | tf_op jit(solution)/shard_map/ppermute | solution.py:28
  37.3 12.0 %collective-permute-start.6 = (bf16[4,192,256]{2,1,0:T(8,128)(2,1)S(1)}, bf16[4,192,256]{2,1,0:T(8,128)(2,1)S(1)}, u32[]{:S(2)}, u32[]{:S(2)}) collective-permute-start(bf16[4,192,256]{2,1,0:T(8,128)(2,1)S(1)} %pad_maximum_fusion.refs_0_), channel_id=1, source_target_pairs={{0,3},{1,0},{2,1},{3,2},{4,7},{5,4},{6,5},{7,6},{8,11},{9,8},{10,9... | collective-permute-start | bytes 1179656 | tf_op jit(solution)/shard_map/ppermute | solution.py:28
  39.5 9.8 %collective-permute-start.4 = (bf16[192,512]{1,0:T(8,128)(2,1)S(1)}, bf16[192,512]{1,0:T(8,128)(2,1)S(1)}, u32[]{:S(2)}, u32[]{:S(2)}) collective-permute-start(bf16[192,512]{1,0:T(8,128)(2,1)S(1)} %constant_dynamic-update-slice_fusion), channel_id=1, source_target_pairs={{0,32},{16,48},{32,0},{48,16},{64,96},{80,112},{96,64},{112,80},{1... | collective-permute-start | bytes 589832 | tf_op jit(solution)/shard_map/ppermute | solution.py:39
  49.3 15.0 %collective-permute-start.10 = (bf16[2,192,512]{2,1,0:T(8,128)(2,1)S(1)}, bf16[2,192,512]{2,1,0:T(8,128)(2,1)S(1)}, u32[]{:S(2)}, u32[]{:S(2)}) collective-permute-start(bf16[2,192,512]{2,1,0:T(8,128)(2,1)S(1)} %pad_maximum_fusion.1.refs_0_), channel_id=1, source_target_pairs={{0,128},{16,144},{32,160},{48,176},{64,192},{80,208},{96,224},{112... | collective-permute-start | bytes 1179656 | tf_op jit(solution)/shard_map/ppermute | solution.py:39
  52.5 18.1 %collective-permute-start.12 = (bf16[2,192,512]{2,1,0:T(8,128)(2,1)S(1)}, bf16[2,192,512]{2,1,0:T(8,128)(2,1)S(1)}, u32[]{:S(2)}, u32[]{:S(2)}) collective-permute-start(bf16[2,192,512]{2,1,0:T(8,128)(2,1)S(1)} %pad_maximum_fusion.1.refs_0_), channel_id=1, source_target_pairs={{0,192},{16,208},{32,224},{48,240},{64,0},{80,16},{96,32},{112,48}... | collective-permute-start | bytes 1179656 | tf_op jit(solution)/shard_map/ppermute | solution.py:39
  53.7 17.0 %collective-permute-start.8 = (bf16[2,192,512]{2,1,0:T(8,128)(2,1)S(1)}, bf16[2,192,512]{2,1,0:T(8,128)(2,1)S(1)}, u32[]{:S(2)}, u32[]{:S(2)}) collective-permute-start(bf16[2,192,512]{2,1,0:T(8,128)(2,1)S(1)} %pad_maximum_fusion.1.refs_0_), channel_id=1, source_target_pairs={{0,64},{16,80},{32,96},{48,112},{64,128},{80,144},{96,160},{112,17... | collective-permute-start | bytes 1179656 | tf_op jit(solution)/shard_map/ppermute | solution.py:39
  54.5 16.6 %collective-permute-start.14 = (bf16[4,192,256]{2,1,0:T(8,128)(2,1)S(1)}, bf16[4,192,256]{2,1,0:T(8,128)(2,1)S(1)}, u32[]{:S(2)}, u32[]{:S(2)}) collective-permute-start(bf16[4,192,256]{2,1,0:T(8,128)(2,1)S(1)} %pad_maximum_fusion.refs_0_), channel_id=1, source_target_pairs={{0,2},{1,3},{2,0},{3,1},{4,6},{5,7},{6,4},{7,5},{8,10},{9,11},{10,... | collective-permute-start | bytes 1179656 | tf_op jit(solution)/shard_map/ppermute | solution.py:28
  56.0 17.4 %collective-permute-start.7 = (bf16[2,192,512]{2,1,0:T(8,128)(2,1)S(1)}, bf16[2,192,512]{2,1,0:T(8,128)(2,1)S(1)}, u32[]{:S(2)}, u32[]{:S(2)}) collective-permute-start(bf16[2,192,512]{2,1,0:T(8,128)(2,1)S(1)} %pad_maximum_fusion.1.refs_0_), channel_id=1, source_target_pairs={{0,16},{16,0},{32,48},{48,32},{64,80},{80,64},{96,112},{112,96},{1... | collective-permute-start | bytes 1179656 | tf_op jit(solution)/shard_map/ppermute | solution.py:39
  64.4 9.1 %collective-permute-start.11 = (bf16[2,192,512]{2,1,0:T(8,128)(2,1)S(1)}, bf16[2,192,512]{2,1,0:T(8,128)(2,1)S(1)}, u32[]{:S(2)}, u32[]{:S(2)}) collective-permute-start(bf16[2,192,512]{2,1,0:T(8,128)(2,1)S(1)} %collective-permute-done.10.refs_2_), channel_id=1, source_target_pairs={{0,16},{16,0},{32,48},{48,32},{64,80},{80,64},{96,112},{112,96},{1... | collective-permute-start | bytes 1179656 | tf_op jit(solution)/shard_map/ppermute | solution.py:39
  84.6 8.5 %collective-permute-start.15 = (bf16[128,256]{1,0:T(8,128)(2,1)S(1)}, bf16[128,256]{1,0:T(8,128)(2,1)S(1)}, u32[]{:S(2)}, u32[]{:S(2)}) collective-permute-start(bf16[128,256]{1,0:T(8,128)(2,1)S(1)} %attend.2.refs_0_), channel_id=1, source_target_pairs={{0,4},{1,5},{2,6},{3,7},{4,8},{5,9},{6,10},{7,11},{8,12},{9,13},{1... | collective-permute-start | bytes 196616 | tf_op jit(solution)/shard_map/ppermute | solution.py:28
  87.9 6.2 %collective-permute-start.16 = (bf16[128,256]{1,0:T(8,128)(2,1)S(1)}, bf16[128,256]{1,0:T(8,128)(2,1)S(1)}, u32[]{:S(2)}, u32[]{:S(2)}) collective-permute-start(bf16[128,256]{1,0:T(8,128)(2,1)S(1)} %attend.2.refs_0_), channel_id=1, source_target_pairs={{0,8},{1,9},{2,10},{3,11},{4,12},{5,13},{6,14},{7,15},{8,0},{9,1},... | collective-permute-start | bytes 196616 | tf_op jit(solution)/shard_map/ppermute | solution.py:28
  95.1 6.2 %collective-permute-start.18 = (bf16[192,256]{1,0:T(8,128)(2,1)S(1)}, bf16[192,256]{1,0:T(8,128)(2,1)S(1)}, u32[]{:S(2)}, u32[]{:S(2)}) collective-permute-start(bf16[192,256]{1,0:T(8,128)(2,1)S(1)} %get-tuple-element.68), channel_id=1, source_target_pairs={{0,1},{1,2},{2,3},{3,0},{4,5},{5,6},{6,7},{7,4},{8,9},{9,10},{10,1... | collective-permute-start | bytes 294920 | tf_op jit(solution)/shard_map/ppermute | solution.py:28
  98.1 6.2 %collective-permute-start.19 = (bf16[192,256]{1,0:T(8,128)(2,1)S(1)}, bf16[192,256]{1,0:T(8,128)(2,1)S(1)}, u32[]{:S(2)}, u32[]{:S(2)}) collective-permute-start(bf16[192,256]{1,0:T(8,128)(2,1)S(1)} %get-tuple-element.69), channel_id=1, source_target_pairs={{0,2},{1,3},{2,0},{3,1},{4,6},{5,7},{6,4},{7,5},{8,10},{9,11},{10,... | collective-permute-start | bytes 294920 | tf_op jit(solution)/shard_map/ppermute | solution.py:28
  98.4 6.9 %collective-permute-start.20 = (bf16[192,256]{1,0:T(8,128)(2,1)S(1)}, bf16[192,256]{1,0:T(8,128)(2,1)S(1)}, u32[]{:S(2)}, u32[]{:S(2)}) collective-permute-start(bf16[192,256]{1,0:T(8,128)(2,1)S(1)} %get-tuple-element.70), channel_id=1, source_target_pairs={{0,3},{1,0},{2,1},{3,2},{4,7},{5,4},{6,5},{7,6},{8,11},{9,8},{10,9... | collective-permute-start | bytes 294920 | tf_op jit(solution)/shard_map/ppermute | solution.py:28
  106.0 7.3 %collective-permute-start.21 = (bf16[192,256]{1,0:T(8,128)(2,1)S(1)}, bf16[192,256]{1,0:T(8,128)(2,1)S(1)}, u32[]{:S(2)}, u32[]{:S(2)}) collective-permute-start(bf16[192,256]{1,0:T(8,128)(2,1)S(1)} %update.2.x), channel_id=1, source_target_pairs={{0,4},{1,5},{2,6},{3,7},{4,8},{5,9},{6,10},{7,11},{8,12},{9,13},{1... | collective-permute-start | bytes 294920 | tf_op jit(solution)/shard_map/ppermute | solution.py:28
  107.7 8.5 %collective-permute-start.22 = (bf16[192,256]{1,0:T(8,128)(2,1)S(1)}, bf16[192,256]{1,0:T(8,128)(2,1)S(1)}, u32[]{:S(2)}, u32[]{:S(2)}) collective-permute-start(bf16[192,256]{1,0:T(8,128)(2,1)S(1)} %update.2.x), channel_id=1, source_target_pairs={{0,8},{1,9},{2,10},{3,11},{4,12},{5,13},{6,14},{7,15},{8,0},{9,1},... | collective-permute-start | bytes 294920 | tf_op jit(solution)/shard_map/ppermute | solution.py:28
  109.8 6.3 %collective-permute-start.23 = (bf16[192,256]{1,0:T(8,128)(2,1)S(1)}, bf16[192,256]{1,0:T(8,128)(2,1)S(1)}, u32[]{:S(2)}, u32[]{:S(2)}) collective-permute-start(bf16[192,256]{1,0:T(8,128)(2,1)S(1)} %update.2.x), channel_id=1, source_target_pairs={{0,12},{1,13},{2,14},{3,15},{4,0},{5,1},{6,2},{7,3},{8,4},{9,5},{1... | collective-permute-start | bytes 294920 | tf_op jit(solution)/shard_map/ppermute | solution.py:28
  116.2 12.3 %collective-permute-start.24 = (bf16[4,192,256]{2,1,0:T(8,128)(2,1)S(1)}, bf16[4,192,256]{2,1,0:T(8,128)(2,1)S(1)}, u32[]{:S(2)}, u32[]{:S(2)}) collective-permute-start(bf16[4,192,256]{2,1,0:T(8,128)(2,1)S(1)} %pad_maximum_fusion.2.refs_0_), channel_id=1, source_target_pairs={{0,1},{1,2},{2,3},{3,0},{4,5},{5,6},{6,7},{7,4},{8,9},{9,10},{10,1... | collective-permute-start | bytes 1179656 | tf_op jit(solution)/shard_map/ppermute | solution.py:28
  117.2 13.6 %collective-permute-start.25 = (bf16[4,192,256]{2,1,0:T(8,128)(2,1)S(1)}, bf16[4,192,256]{2,1,0:T(8,128)(2,1)S(1)}, u32[]{:S(2)}, u32[]{:S(2)}) collective-permute-start(bf16[4,192,256]{2,1,0:T(8,128)(2,1)S(1)} %pad_maximum_fusion.2.refs_0_), channel_id=1, source_target_pairs={{0,2},{1,3},{2,0},{3,1},{4,6},{5,7},{6,4},{7,5},{8,10},{9,11},{10,... | collective-permute-start | bytes 1179656 | tf_op jit(solution)/shard_map/ppermute | solution.py:28
  118.1 18.9 %collective-permute-start.26 = (bf16[4,192,256]{2,1,0:T(8,128)(2,1)S(1)}, bf16[4,192,256]{2,1,0:T(8,128)(2,1)S(1)}, u32[]{:S(2)}, u32[]{:S(2)}) collective-permute-start(bf16[4,192,256]{2,1,0:T(8,128)(2,1)S(1)} %pad_maximum_fusion.2.refs_0_), channel_id=1, source_target_pairs={{0,3},{1,0},{2,1},{3,2},{4,7},{5,4},{6,5},{7,6},{8,11},{9,8},{10,9... | collective-permute-start | bytes 1179656 | tf_op jit(solution)/shard_map/ppermute | solution.py:28
  150.8 6.9 %collective-permute-start.27 = (bf16[128,256]{1,0:T(8,128)(2,1)S(1)}, bf16[128,256]{1,0:T(8,128)(2,1)S(1)}, u32[]{:S(2)}, u32[]{:S(2)}) collective-permute-start(bf16[128,256]{1,0:T(8,128)(2,1)S(1)} %attend.3.refs_0_), channel_id=1, source_target_pairs={{0,4},{1,5},{2,6},{3,7},{4,8},{5,9},{6,10},{7,11},{8,12},{9,13},{1... | collective-permute-start | bytes 196616 | tf_op jit(solution)/shard_map/ppermute | solution.py:28
  151.5 8.3 %collective-permute-start.28 = (bf16[128,256]{1,0:T(8,128)(2,1)S(1)}, bf16[128,256]{1,0:T(8,128)(2,1)S(1)}, u32[]{:S(2)}, u32[]{:S(2)}) collective-permute-start(bf16[128,256]{1,0:T(8,128)(2,1)S(1)} %attend.3.refs_0_), channel_id=1, source_target_pairs={{0,8},{1,9},{2,10},{3,11},{4,12},{5,13},{6,14},{7,15},{8,0},{9,1},... | collective-permute-start | bytes 196616 | tf_op jit(solution)/shard_map/ppermute | solution.py:28
  151.5 8.3 %collective-permute-start.29 = (bf16[128,256]{1,0:T(8,128)(2,1)S(1)}, bf16[128,256]{1,0:T(8,128)(2,1)S(1)}, u32[]{:S(2)}, u32[]{:S(2)}) collective-permute-start(bf16[128,256]{1,0:T(8,128)(2,1)S(1)} %attend.3.refs_0_), channel_id=1, source_target_pairs={{0,12},{1,13},{2,14},{3,15},{4,0},{5,1},{6,2},{7,3},{8,4},{9,5},{1... | collective-permute-start | bytes 196616 | tf_op jit(solution)/shard_map/ppermute | solution.py:28
  161.4 6.4 %collective-permute-start.31 = (bf16[192,256]{1,0:T(8,128)(2,1)S(1)}, bf16[192,256]{1,0:T(8,128)(2,1)S(1)}, u32[]{:S(2)}, u32[]{:S(2)}) collective-permute-start(bf16[192,256]{1,0:T(8,128)(2,1)S(1)} %get-tuple-element.79), channel_id=1, source_target_pairs={{0,2},{1,3},{2,0},{3,1},{4,6},{5,7},{6,4},{7,5},{8,10},{9,11},{10,... | collective-permute-start | bytes 294920 | tf_op jit(solution)/shard_map/ppermute | solution.py:28
  163.7 5.8 %collective-permute-start.32 = (bf16[192,256]{1,0:T(8,128)(2,1)S(1)}, bf16[192,256]{1,0:T(8,128)(2,1)S(1)}, u32[]{:S(2)}, u32[]{:S(2)}) collective-permute-start(bf16[192,256]{1,0:T(8,128)(2,1)S(1)} %get-tuple-element.80), channel_id=1, source_target_pairs={{0,3},{1,0},{2,1},{3,2},{4,7},{5,4},{6,5},{7,6},{8,11},{9,8},{10,9... | collective-permute-start | bytes 294920 | tf_op jit(solution)/shard_map/ppermute | solution.py:28
  (18 other events, 240.1 us)
Sparse Core Ops, SparseCore 0:
  10.7 69.8 all-gather.3
  83.2 62.5 all-gather.5
where the time goes:
time: 179 us
  waiting for transfers between devices  77.6 us (43%)
  starting transfers between devices  57.3 us (32%)
  Pallas kernels  19.6 us (11%)
  between operations  14.3 us (8%)
  local copies, waits for them, and re-layouts  8.81 us (5%)
    ppermute x24, waiting for transfers between devices, shift(): return lax.ppermute(array, 'tp', pairs)  42.2 us
    ppermute x24, starting transfers between devices, shift(): return lax.ppermute(array, 'tp', pairs)  34.2 us
    ppermute x8, waiting for transfers between devices, shift(): return lax.ppermute(array, 'patch', pairs)  20.5 us
    pallas_call x11, Pallas kernels, call(): pl.pallas_call(body, out_shape=outs, in_specs=[pl.BlockSpec(memory_space=...  19.6 us
    ppermute x8, starting transfers between devices, shift(): return lax.ppermute(array, 'patch', pairs)  9.69 us
    all_to_all x1, starting transfers between devices, on_device(): w_mine = lax.all_to_all(sent, 'tp', 0, 0)  8.85 us
    unnamed x30, local copies, waits for them, and re-layouts  6.72 us
    ppermute x1, waiting for transfers between devices, swap(): return lax.ppermute(array, ('patch', 'tp'), pairs)  6.64 us
  transfers between devices with their start and end apart: 36, of which 21 were waited for; matrix products, arithmetic and copies ran while one was open for 2% of the time, Pallas kernels for 8%

commit v1 on v0

--- a/solution.py
+++ b/solution.py
@@ -229,13 +229,17 @@
     x_up, x_down = shift(x_four, "x", 1), shift(x_four, "x", 3)
     w_h, x_up, x_down = sync(w_h, x_up, x_down)
     w_pair = jnp.stack([w_mine, w_h])
-    w_quad = [w_pair] + shifts(w_pair, "y", NY)
+    w_up, w_down = shift(w_pair, "y", 1), shift(w_pair, "y", 3)
     x_far = shift(x_four, "x", 2)
+    w_up, w_down, w_pair = sync(w_up, w_down, w_pair)
+    w_far = [shift(w_up[:1], "y", 1), shift(w_down[1:], "y", 3)]
+    w_quad = [w_pair, w_up, *w_far, w_down]
     w_c = [shift(piece, "c", 1) for piece in w_quad]
     normed = norm(0, [x_four, x_up, x_far, x_down])
     w_c, w_quad, normed = sync(w_c, w_quad, normed)
     past = cache_all
-    weights, w_table = w_quad + w_c, [NH * k for k in range(NC * NY)]
+    weights = w_quad + w_c
+    w_table = [place + NY * NH * kc for kc in range(NC) for place in (0, NH, 2 * NH, 2 * NH + 1, 3 * NH)]
     for step in range(STEPS):
         last = step + 1 == STEPS
         kv, near = call(

time: 179 us -> 178 us (level)
  waiting for transfers between devices: 77.6 us -> 75.7 us
    ppermute x8 -> x10, waiting for transfers between devices: 20.5 us -> 17.8 us  [shift(): return lax.ppermute(array, 'patch', pairs)]
    ppermute x8 -> x10, starting transfers between devices: 9.69 us -> 11.8 us  [shift(): return lax.ppermute(array, 'patch', pairs)]
    unnamed x30 -> x28, local copies, waits for them, and re-layouts: 6.72 us -> 5.76 us
  transfers between devices with their start and end apart: 36 -> 38, of which waited for: 21 -> 20; matrix products, arithmetic and copies ran while one was open for 2% -> 2% of each run, Pallas kernels for 8% -> 8%
where the time goes in v1:
time: 178 us; the launch traced here: 177 us
  waiting for transfers between devices  75.7 us (43%)
  starting transfers between devices  58.6 us (33%)
  Pallas kernels  19.6 us (11%)
  between operations  14.3 us (8%)
  local copies, waits for them, and re-layouts  7.88 us (4%)
    ppermute x24, waiting for transfers between devices, shift(): return lax.ppermute(array, 'tp', pairs)  42.6 us
    ppermute x24, starting transfers between devices, shift(): return lax.ppermute(array, 'tp', pairs)  33.5 us
    pallas_call x11, Pallas kernels, call(): pl.pallas_call(body, out_shape=outs, in_specs=[pl.BlockSpec(memory_space=...  19.6 us
    ppermute x10, waiting for transfers between devices, shift(): return lax.ppermute(array, 'patch', pairs)  17.8 us
    ppermute x10, starting transfers between devices, shift(): return lax.ppermute(array, 'patch', pairs)  11.8 us
    all_to_all x1, starting transfers between devices, on_device(): w_mine = lax.all_to_all(sent, 'tp', 0, 0)  8.85 us
    ppermute x1, waiting for transfers between devices, swap(): return lax.ppermute(array, ('patch', 'tp'), pairs)  6.65 us
    unnamed x28, local copies, waits for them, and re-layouts  5.76 us
  transfers between devices with their start and end apart: 38, of which 20 were waited for; matrix products, arithmetic and copies ran while one was open for 2% of the time, Pallas kernels for 8%

profile of v1, /device:TPU:6, one launch (start us, length us, event | category | flops | bytes accessed | tf_op | source)
XLA Modules:
  0.0 177.3 jit_solution(16634578247860139661)
XLA Ops:
  9.7 8.9 %all-to-all-start = ((bf16[16,36,128]{2,1,0:T(8,128)(2,1)}), bf16[16,36,128]{2,1,0:T(8,128)(2,1)S(1)}, u32[]{:S(2)}, u32[]{:S(2)}) async-start(bf16[16,36,128]{2,1,0:T(8,128)(2,1)} %copy.14), calls=%async_computation | async-start | bytes 327680 | tf_op jit(solution)/shard_map/all_to_all | solution.py:220
  20.2 2.4 %collective-permute-start.1 = (bf16[192,256]{1,0:T(8,128)(2,1)}, bf16[192,256]{1,0:T(8,128)(2,1)S(1)}, u32[]{:S(2)}, u32[]{:S(2)}) collective-permute-start(bf16[192,256]{1,0:T(8,128)(2,1)} %bitcast.32), channel_id=1, source_target_pairs={{0,8},{1,9},{2,10},{3,11},{4,12},{5,13},{6,14},{7,15},{8,0},{9,1},... | collective-permute-start | bytes 294920 | tf_op jit(solution)/shard_map/ppermute | solution.py:28
  24.0 4.4 %collective-permute-start.3 = (bf16[192,128]{1,0:T(8,128)(2,1)}, bf16[192,128]{1,0:T(8,128)(2,1)S(1)}, u32[]{:S(2)}, u32[]{:S(2)}) collective-permute-start(bf16[192,128]{1,0:T(8,128)(2,1)} %param.11), channel_id=1, source_target_pairs={{0,0},{1,16},{2,32},{3,48},{4,4},{5,20},{6,36},{7,52},{8,8},{9,24}... | collective-permute-start | bytes 147464 | tf_op jit(solution)/shard_map/ppermute | solution.py:192
  29.5 6.7 %collective-permute-done.3 = bf16[192,128]{1,0:T(8,128)(2,1)S(1)} collective-permute-done((bf16[192,128]{1,0:T(8,128)(2,1)}, bf16[192,128]{1,0:T(8,128)(2,1)S(1)}, u32[]{:S(2)}, u32[]{:S(2)}) %collective-permute-start.3) | collective-permute-done | bytes 49184 | tf_op jit(solution)/shard_map/ppermute | solution.py:192
  39.5 4.0 %collective-permute-start.4 = (bf16[192,512]{1,0:T(8,128)(2,1)S(1)}, bf16[192,512]{1,0:T(8,128)(2,1)S(1)}, u32[]{:S(2)}, u32[]{:S(2)}) collective-permute-start(bf16[192,512]{1,0:T(8,128)(2,1)S(1)} %constant_dynamic-update-slice_fusion), channel_id=1, source_target_pairs={{0,32},{16,48},{32,0},{48,16},{64,96},{80,112},{96,64},{112,80},{1... | collective-permute-start | bytes 589832 | tf_op jit(solution)/shard_map/ppermute | solution.py:39
  43.4 5.8 %collective-permute-done.4 = bf16[192,512]{1,0:T(8,128)(2,1)S(1)} collective-permute-done((bf16[192,512]{1,0:T(8,128)(2,1)S(1)}, bf16[192,512]{1,0:T(8,128)(2,1)S(1)}, u32[]{:S(2)}, u32[]{:S(2)}) %collective-permute-start.4) | collective-permute-done | bytes 196640 | tf_op jit(solution)/shard_map/ppermute | solution.py:39
  54.0 6.5 %collective-permute-done.7.refs_1_ = bf16[2,192,512]{2,1,0:T(8,128)(2,1)S(1)} collective-permute-done((bf16[2,192,512]{2,1,0:T(8,128)(2,1)S(1)}, bf16[2,192,512]{2,1,0:T(8,128)(2,1)S(1)}, u32[]{:S(2)}, u32[]{:S(2)}) %collective-permute-start.7) | collective-permute-done | bytes 393248 | tf_op jit(solution)/shard_map/ppermute | solution.py:39
  64.6 5.4 %collective-permute-done.11.refs_2_ = bf16[1,192,512]{2,1,0:T(8,128)(2,1)S(1)} collective-permute-done((bf16[1,192,512]{2,1,0:T(8,128)(2,1)S(1)}, bf16[1,192,512]{2,1,0:T(8,128)(2,1)S(1)}, u32[]{:S(2)}, u32[]{:S(2)}) %collective-permute-start.11) | collective-permute-done | bytes 196640 | tf_op jit(solution)/shard_map/ppermute | solution.py:39
  70.5 2.2 %norm.2.normed = bf16[16,192,256]{2,1,0:T(8,128)(2,1)S(1)} custom-call(s32[2]{0:T(128)S(1)} %pad_add_fusion.ids, f32[96,192]{1,0:T(8,128)S(1)} %reshape.30.mod, bf16[4,192,256]{2,1,0:T(8,128)(2,1)S(1)} %pad_maximum_fusion.refs_0_, bf16[4,192,256]{2,1,0:T(8,128)(2,1)S(1)} %collective-permute-done.5.refs_1_, ...), custom_call_target="tpu_custom_call" | custom-call | flops 1048576 | bytes 4194304 | tf_op jit(solution)/shard_map/norm/pallas_call | solution.py:53
  72.8 2.7 %qkv.2 = (bf16[512,128]{1,0:T(8,128)(2,1)}, bf16[768,128]{1,0:T(8,128)(2,1)S(1)}) custom-call(s32[2]{0:T(128)S(1)} %pad_add_fusion.ids, bf16[16,192,256]{2,1,0:T(8,128)(2,1)S(1)} %norm.2.normed, f32[1,128]{1,0:T(1,128)S(1)} %bitcast.36, f32[1,128]{1,0:T(1,128)S(1)} %bitcast.38, bf16[2,192,512]{2,1,0:T(8,128)(2,1)S(1)} %pad_maximum_fusion.1.refs_0_, ...), custom_call_target="tpu_custom_call" | custom-call | flops 1048576 | bytes 16777216 | tf_op jit(solution)/shard_map/qkv/pallas_call | solution.py:53
  75.5 5.0 %all-gather.4.cloned.1.call-done.past = bf16[16,512,128]{2,1,0:T(8,128)(2,1)} async-done(((bf16[1,512,128]{2,1,0:T(8,128)(2,1)}), bf16[16,512,128]{2,1,0:T(8,128)(2,1)}) %all-gather.4.cloned.1.call-update) | async-done | bytes 2097168 | tf_op jit(solution)/shard_map/all_gather | solution.py:222
  82.1 2.4 %attend.2.refs_0_ = bf16[128,256]{1,0:T(8,128)(2,1)S(1)} custom-call(s32[2]{0:T(128)S(1)} %pad_add_fusion.ids, bf16[768,128]{1,0:T(8,128)(2,1)S(1)} %get-tuple-element.72.near, bf16[16,512,128]{2,1,0:T(8,128)(2,1)S(1)} %copy-done), custom_call_target="tpu_custom_call" | custom-call | flops 1048576 | bytes 8388608 | tf_op jit(solution)/shard_map/attend/pallas_call | solution.py:53
  84.6 2.1 %collective-permute-start.17 = (bf16[128,256]{1,0:T(8,128)(2,1)S(1)}, bf16[128,256]{1,0:T(8,128)(2,1)S(1)}, u32[]{:S(2)}, u32[]{:S(2)}) collective-permute-start(bf16[128,256]{1,0:T(8,128)(2,1)S(1)} %attend.2.refs_0_), channel_id=1, source_target_pairs={{0,4},{1,5},{2,6},{3,7},{4,8},{5,9},{6,10},{7,11},{8,12},{9,13},{1... | collective-permute-start | bytes 196616 | tf_op jit(solution)/shard_map/ppermute | solution.py:28
  88.5 2.8 %collective-permute-start.19 = (bf16[128,256]{1,0:T(8,128)(2,1)S(1)}, bf16[128,256]{1,0:T(8,128)(2,1)S(1)}, u32[]{:S(2)}, u32[]{:S(2)}) collective-permute-start(bf16[128,256]{1,0:T(8,128)(2,1)S(1)} %attend.2.refs_0_), channel_id=1, source_target_pairs={{0,12},{1,13},{2,14},{3,15},{4,0},{5,1},{6,2},{7,3},{8,4},{9,5},{1... | collective-permute-start | bytes 196616 | tf_op jit(solution)/shard_map/ppermute | solution.py:28
  94.5 2.8 %collective-permute-start.20 = (bf16[192,256]{1,0:T(8,128)(2,1)S(1)}, bf16[192,256]{1,0:T(8,128)(2,1)S(1)}, u32[]{:S(2)}, u32[]{:S(2)}) collective-permute-start(bf16[192,256]{1,0:T(8,128)(2,1)S(1)} %get-tuple-element.78), channel_id=1, source_target_pairs={{0,1},{1,2},{2,3},{3,0},{4,5},{5,6},{6,7},{7,4},{8,9},{9,10},{10,1... | collective-permute-start | bytes 294920 | tf_op jit(solution)/shard_map/ppermute | solution.py:28
  98.3 2.6 %collective-permute-done.20.refs_0_ = bf16[192,256]{1,0:T(8,128)(2,1)S(1)} collective-permute-done((bf16[192,256]{1,0:T(8,128)(2,1)S(1)}, bf16[192,256]{1,0:T(8,128)(2,1)S(1)}, u32[]{:S(2)}, u32[]{:S(2)}) %collective-permute-start.20) | collective-permute-done | bytes 98336 | tf_op jit(solution)/shard_map/ppermute | solution.py:28
  100.9 2.6 %collective-permute-done.21.refs_1_ = bf16[192,256]{1,0:T(8,128)(2,1)S(1)} collective-permute-done((bf16[192,256]{1,0:T(8,128)(2,1)S(1)}, bf16[192,256]{1,0:T(8,128)(2,1)S(1)}, u32[]{:S(2)}, u32[]{:S(2)}) %collective-permute-start.21) | collective-permute-done | bytes 98336 | tf_op jit(solution)/shard_map/ppermute | solution.py:28
  107.4 2.1 %collective-permute-start.24 = (bf16[192,256]{1,0:T(8,128)(2,1)S(1)}, bf16[192,256]{1,0:T(8,128)(2,1)S(1)}, u32[]{:S(2)}, u32[]{:S(2)}) collective-permute-start(bf16[192,256]{1,0:T(8,128)(2,1)S(1)} %update.2.x), channel_id=1, source_target_pairs={{0,8},{1,9},{2,10},{3,11},{4,12},{5,13},{6,14},{7,15},{8,0},{9,1},... | collective-permute-start | bytes 294920 | tf_op jit(solution)/shard_map/ppermute | solution.py:28
  109.9 3.1 %collective-permute-done.23 = bf16[192,256]{1,0:T(8,128)(2,1)S(1)} collective-permute-done((bf16[192,256]{1,0:T(8,128)(2,1)S(1)}, bf16[192,256]{1,0:T(8,128)(2,1)S(1)}, u32[]{:S(2)}, u32[]{:S(2)}) %collective-permute-start.23) | collective-permute-done | bytes 98336 | tf_op jit(solution)/shard_map/ppermute | solution.py:28
  113.0 2.6 %collective-permute-done.24 = bf16[192,256]{1,0:T(8,128)(2,1)S(1)} collective-permute-done((bf16[192,256]{1,0:T(8,128)(2,1)S(1)}, bf16[192,256]{1,0:T(8,128)(2,1)S(1)}, u32[]{:S(2)}, u32[]{:S(2)}) %collective-permute-start.24) | collective-permute-done | bytes 98336 | tf_op jit(solution)/shard_map/ppermute | solution.py:28
  116.1 2.2 %collective-permute-start.27 = (bf16[4,192,256]{2,1,0:T(8,128)(2,1)S(1)}, bf16[4,192,256]{2,1,0:T(8,128)(2,1)S(1)}, u32[]{:S(2)}, u32[]{:S(2)}) collective-permute-start(bf16[4,192,256]{2,1,0:T(8,128)(2,1)S(1)} %pad_maximum_fusion.2.refs_0_), channel_id=1, source_target_pairs={{0,2},{1,3},{2,0},{3,1},{4,6},{5,7},{6,4},{7,5},{8,10},{9,11},{10,... | collective-permute-start | bytes 1179656 | tf_op jit(solution)/shard_map/ppermute | solution.py:28
  118.3 9.7 %collective-permute-done.26.refs_1_ = bf16[4,192,256]{2,1,0:T(8,128)(2,1)S(1)} collective-permute-done((bf16[4,192,256]{2,1,0:T(8,128)(2,1)S(1)}, bf16[4,192,256]{2,1,0:T(8,128)(2,1)S(1)}, u32[]{:S(2)}, u32[]{:S(2)}) %collective-permute-start.26) | collective-permute-done | bytes 393248 | tf_op jit(solution)/shard_map/ppermute | solution.py:28
  129.7 7.1 %collective-permute-done.28.refs_3_ = bf16[4,192,256]{2,1,0:T(8,128)(2,1)S(1)} collective-permute-done((bf16[4,192,256]{2,1,0:T(8,128)(2,1)S(1)}, bf16[4,192,256]{2,1,0:T(8,128)(2,1)S(1)}, u32[]{:S(2)}, u32[]{:S(2)}) %collective-permute-start.28) | collective-permute-done | bytes 393248 | tf_op jit(solution)/shard_map/ppermute | solution.py:28
  136.7 2.2 %norm.3.normed = bf16[16,192,256]{2,1,0:T(8,128)(2,1)S(1)} custom-call(s32[2]{0:T(128)S(1)} %pad_add_fusion.ids, f32[96,192]{1,0:T(8,128)S(1)} %reshape.30.mod, bf16[4,192,256]{2,1,0:T(8,128)(2,1)S(1)} %pad_maximum_fusion.2.refs_0_, bf16[4,192,256]{2,1,0:T(8,128)(2,1)S(1)} %collective-permute-done.26.refs_1_, ...), custom_call_target="tpu_custom_call" | custom-call | flops 1048576 | bytes 4194304 | tf_op jit(solution)/shard_map/norm/pallas_call | solution.py:53
  139.0 2.7 %qkv.3 = (bf16[512,128]{1,0:T(8,128)(2,1)}, bf16[768,128]{1,0:T(8,128)(2,1)S(1)}) custom-call(s32[2]{0:T(128)S(1)} %pad_add_fusion.ids, bf16[16,192,256]{2,1,0:T(8,128)(2,1)S(1)} %norm.3.normed, f32[1,128]{1,0:T(1,128)S(1)} %bitcast.37, f32[1,128]{1,0:T(1,128)S(1)} %bitcast.39, bf16[2,192,512]{2,1,0:T(8,128)(2,1)S(1)} %pad_maximum_fusion.1.refs_0_, ...), custom_call_target="tpu_custom_call" | custom-call | flops 1048576 | bytes 16777216 | tf_op jit(solution)/shard_map/qkv/pallas_call | solution.py:53
  142.3 3.0 %all-gather.6.cloned.1.call-done = bf16[8192,128]{1,0:T(8,128)(2,1)} async-done(((bf16[512,128]{1,0:T(8,128)(2,1)}), bf16[8192,128]{1,0:T(8,128)(2,1)}) %all-gather.6.cloned.1.call-update) | async-done | bytes 2097168 | tf_op jit(solution)/shard_map/all_gather | solution.py:255
  147.9 2.4 %attend.3.refs_0_ = bf16[128,256]{1,0:T(8,128)(2,1)S(1)} custom-call(s32[2]{0:T(128)S(1)} %pad_add_fusion.ids, bf16[768,128]{1,0:T(8,128)(2,1)S(1)} %copy-done.10, bf16[16,512,128]{2,1,0:T(8,128)(2,1)S(1)} %bitcast.29), custom_call_target="tpu_custom_call" | custom-call | flops 1048576 | bytes 8388608 | tf_op jit(solution)/shard_map/attend/pallas_call | solution.py:53
  151.0 3.2 %collective-permute-start.31 = (bf16[128,256]{1,0:T(8,128)(2,1)S(1)}, bf16[128,256]{1,0:T(8,128)(2,1)S(1)}, u32[]{:S(2)}, u32[]{:S(2)}) collective-permute-start(bf16[128,256]{1,0:T(8,128)(2,1)S(1)} %attend.3.refs_0_), channel_id=1, source_target_pairs={{0,12},{1,13},{2,14},{3,15},{4,0},{5,1},{6,2},{7,3},{8,4},{9,5},{1... | collective-permute-start | bytes 196616 | tf_op jit(solution)/shard_map/ppermute | solution.py:28
  154.2 3.0 %collective-permute-done.29.refs_1_ = bf16[128,256]{1,0:T(8,128)(2,1)S(1)} collective-permute-done((bf16[128,256]{1,0:T(8,128)(2,1)S(1)}, bf16[128,256]{1,0:T(8,128)(2,1)S(1)}, u32[]{:S(2)}, u32[]{:S(2)}) %collective-permute-start.29) | collective-permute-done | bytes 65568 | tf_op jit(solution)/shard_map/ppermute | solution.py:28
  157.2 2.1 %collective-permute-done.30.refs_2_ = bf16[128,256]{1,0:T(8,128)(2,1)S(1)} collective-permute-done((bf16[128,256]{1,0:T(8,128)(2,1)S(1)}, bf16[128,256]{1,0:T(8,128)(2,1)S(1)}, u32[]{:S(2)}, u32[]{:S(2)}) %collective-permute-start.30) | collective-permute-done | bytes 65568 | tf_op jit(solution)/shard_map/ppermute | solution.py:28
  160.9 2.4 %collective-permute-start.33 = (bf16[192,256]{1,0:T(8,128)(2,1)S(1)}, bf16[192,256]{1,0:T(8,128)(2,1)S(1)}, u32[]{:S(2)}, u32[]{:S(2)}) collective-permute-start(bf16[192,256]{1,0:T(8,128)(2,1)S(1)} %get-tuple-element.89), channel_id=1, source_target_pairs={{0,2},{1,3},{2,0},{3,1},{4,6},{5,7},{6,4},{7,5},{8,10},{9,11},{10,... | collective-permute-start | bytes 294920 | tf_op jit(solution)/shard_map/ppermute | solution.py:28
  164.9 2.4 %collective-permute-done.33.refs_1_ = bf16[192,256]{1,0:T(8,128)(2,1)S(1)} collective-permute-done((bf16[192,256]{1,0:T(8,128)(2,1)S(1)}, bf16[192,256]{1,0:T(8,128)(2,1)S(1)}, u32[]{:S(2)}, u32[]{:S(2)}) %collective-permute-start.33) | collective-permute-done | bytes 98336 | tf_op jit(solution)/shard_map/ppermute | solution.py:28
  (98 shorter events, 43.6 us)
Async XLA Ops:
  7.2 73.4 %all-gather.4.cloned.1.call-start = ((), (), s32[]{:S(2)}) async-start(), calls=%async_computation.1 | async-start | bytes 2228224 | tf_op jit(solution)/shard_map/all_gather | solution.py:222
  9.7 26.5 %all-to-all-start = ((bf16[16,36,128]{2,1,0:T(8,128)(2,1)}), bf16[16,36,128]{2,1,0:T(8,128)(2,1)S(1)}, u32[]{:S(2)}, u32[]{:S(2)}) async-start(bf16[16,36,128]{2,1,0:T(8,128)(2,1)} %copy.14), calls=%async_computation | async-start | bytes 327680 | tf_op jit(solution)/shard_map/all_to_all | solution.py:220
  18.6 126.8 %all-gather.6.cloned.1.call-start = ((), (), s32[]{:S(2)}) async-start(), calls=%async_computation.2 | async-start | bytes 2228224 | tf_op jit(solution)/shard_map/all_gather | solution.py:255
  18.6 17.6 %collective-permute-start = (bf16[192,256]{1,0:T(8,128)(2,1)}, bf16[192,256]{1,0:T(8,128)(2,1)S(1)}, u32[]{:S(2)}, u32[]{:S(2)}) collective-permute-start(bf16[192,256]{1,0:T(8,128)(2,1)} %bitcast.31), channel_id=1, source_target_pairs={{0,4},{1,5},{2,6},{3,7},{4,8},{5,9},{6,10},{7,11},{8,12},{9,13},{1... | collective-permute-start | bytes 294920 | tf_op jit(solution)/shard_map/ppermute | solution.py:28
  20.2 16.0 %collective-permute-start.1 = (bf16[192,256]{1,0:T(8,128)(2,1)}, bf16[192,256]{1,0:T(8,128)(2,1)S(1)}, u32[]{:S(2)}, u32[]{:S(2)}) collective-permute-start(bf16[192,256]{1,0:T(8,128)(2,1)} %bitcast.32), channel_id=1, source_target_pairs={{0,8},{1,9},{2,10},{3,11},{4,12},{5,13},{6,14},{7,15},{8,0},{9,1},... | collective-permute-start | bytes 294920 | tf_op jit(solution)/shard_map/ppermute | solution.py:28
  22.5 13.7 %collective-permute-start.2 = (bf16[192,256]{1,0:T(8,128)(2,1)}, bf16[192,256]{1,0:T(8,128)(2,1)S(1)}, u32[]{:S(2)}, u32[]{:S(2)}) collective-permute-start(bf16[192,256]{1,0:T(8,128)(2,1)} %bitcast.33), channel_id=1, source_target_pairs={{0,12},{1,13},{2,14},{3,15},{4,0},{5,1},{6,2},{7,3},{8,4},{9,5},{1... | collective-permute-start | bytes 294920 | tf_op jit(solution)/shard_map/ppermute | solution.py:28
  24.0 12.2 %collective-permute-start.3 = (bf16[192,128]{1,0:T(8,128)(2,1)}, bf16[192,128]{1,0:T(8,128)(2,1)S(1)}, u32[]{:S(2)}, u32[]{:S(2)}) collective-permute-start(bf16[192,128]{1,0:T(8,128)(2,1)} %param.11), channel_id=1, source_target_pairs={{0,0},{1,16},{2,32},{3,48},{4,4},{5,20},{6,36},{7,52},{8,8},{9,24}... | collective-permute-start | bytes 147464 | tf_op jit(solution)/shard_map/ppermute | solution.py:192
  37.2 12.1 %collective-permute-start.5 = (bf16[4,192,256]{2,1,0:T(8,128)(2,1)S(1)}, bf16[4,192,256]{2,1,0:T(8,128)(2,1)S(1)}, u32[]{:S(2)}, u32[]{:S(2)}) collective-permute-start(bf16[4,192,256]{2,1,0:T(8,128)(2,1)S(1)} %pad_maximum_fusion.refs_0_), channel_id=1, source_target_pairs={{0,1},{1,2},{2,3},{3,0},{4,5},{5,6},{6,7},{7,4},{8,9},{9,10},{10,1... | collective-permute-start | bytes 1179656 | tf_op jit(solution)/shard_map/ppermute | solution.py:28
  37.3 12.0 %collective-permute-start.6 = (bf16[4,192,256]{2,1,0:T(8,128)(2,1)S(1)}, bf16[4,192,256]{2,1,0:T(8,128)(2,1)S(1)}, u32[]{:S(2)}, u32[]{:S(2)}) collective-permute-start(bf16[4,192,256]{2,1,0:T(8,128)(2,1)S(1)} %pad_maximum_fusion.refs_0_), channel_id=1, source_target_pairs={{0,3},{1,0},{2,1},{3,2},{4,7},{5,4},{6,5},{7,6},{8,11},{9,8},{10,9... | collective-permute-start | bytes 1179656 | tf_op jit(solution)/shard_map/ppermute | solution.py:28
  39.5 9.8 %collective-permute-start.4 = (bf16[192,512]{1,0:T(8,128)(2,1)S(1)}, bf16[192,512]{1,0:T(8,128)(2,1)S(1)}, u32[]{:S(2)}, u32[]{:S(2)}) collective-permute-start(bf16[192,512]{1,0:T(8,128)(2,1)S(1)} %constant_dynamic-update-slice_fusion), channel_id=1, source_target_pairs={{0,32},{16,48},{32,0},{48,16},{64,96},{80,112},{96,64},{112,80},{1... | collective-permute-start | bytes 589832 | tf_op jit(solution)/shard_map/ppermute | solution.py:39
  49.3 11.2 %collective-permute-start.7 = (bf16[2,192,512]{2,1,0:T(8,128)(2,1)S(1)}, bf16[2,192,512]{2,1,0:T(8,128)(2,1)S(1)}, u32[]{:S(2)}, u32[]{:S(2)}) collective-permute-start(bf16[2,192,512]{2,1,0:T(8,128)(2,1)S(1)} %pad_maximum_fusion.1.refs_0_), channel_id=1, source_target_pairs={{0,64},{16,80},{32,96},{48,112},{64,128},{80,144},{96,160},{112,17... | collective-permute-start | bytes 1179656 | tf_op jit(solution)/shard_map/ppermute | solution.py:39
  51.0 9.6 %collective-permute-start.8 = (bf16[2,192,512]{2,1,0:T(8,128)(2,1)S(1)}, bf16[2,192,512]{2,1,0:T(8,128)(2,1)S(1)}, u32[]{:S(2)}, u32[]{:S(2)}) collective-permute-start(bf16[2,192,512]{2,1,0:T(8,128)(2,1)S(1)} %pad_maximum_fusion.1.refs_0_), channel_id=1, source_target_pairs={{0,192},{16,208},{32,224},{48,240},{64,0},{80,16},{96,32},{112,48}... | collective-permute-start | bytes 1179656 | tf_op jit(solution)/shard_map/ppermute | solution.py:39
  52.6 11.5 %collective-permute-start.16 = (bf16[4,192,256]{2,1,0:T(8,128)(2,1)S(1)}, bf16[4,192,256]{2,1,0:T(8,128)(2,1)S(1)}, u32[]{:S(2)}, u32[]{:S(2)}) collective-permute-start(bf16[4,192,256]{2,1,0:T(8,128)(2,1)S(1)} %pad_maximum_fusion.refs_0_), channel_id=1, source_target_pairs={{0,2},{1,3},{2,0},{3,1},{4,6},{5,7},{6,4},{7,5},{8,10},{9,11},{10,... | collective-permute-start | bytes 1179656 | tf_op jit(solution)/shard_map/ppermute | solution.py:28
  60.6 12.2 %collective-permute-start.10 = (bf16[2,192,512]{2,1,0:T(8,128)(2,1)S(1)}, bf16[2,192,512]{2,1,0:T(8,128)(2,1)S(1)}, u32[]{:S(2)}, u32[]{:S(2)}) collective-permute-start(bf16[2,192,512]{2,1,0:T(8,128)(2,1)S(1)} %collective-permute-done.7.refs_1_), channel_id=1, source_target_pairs={{0,16},{16,0},{32,48},{48,32},{64,80},{80,64},{96,112},{112,96},{1... | collective-permute-start | bytes 1179656 | tf_op jit(solution)/shard_map/ppermute | solution.py:39
  60.7 9.3 %collective-permute-start.11 = (bf16[1,192,512]{2,1,0:T(8,128)(2,1)S(1)}, bf16[1,192,512]{2,1,0:T(8,128)(2,1)S(1)}, u32[]{:S(2)}, u32[]{:S(2)}) collective-permute-start(bf16[1,192,512]{2,1,0:T(8,128)(2,1)S(1)} %slice.6), channel_id=1, source_target_pairs={{0,64},{16,80},{32,96},{48,112},{64,128},{80,144},{96,160},{112,17... | collective-permute-start | bytes 589832 | tf_op jit(solution)/shard_map/ppermute | solution.py:39
  62.2 7.8 %collective-permute-start.13 = (bf16[1,192,512]{2,1,0:T(8,128)(2,1)S(1)}, bf16[1,192,512]{2,1,0:T(8,128)(2,1)S(1)}, u32[]{:S(2)}, u32[]{:S(2)}) collective-permute-start(bf16[1,192,512]{2,1,0:T(8,128)(2,1)S(1)} %slice.7), channel_id=1, source_target_pairs={{0,192},{16,208},{32,224},{48,240},{64,0},{80,16},{96,32},{112,48}... | collective-permute-start | bytes 589832 | tf_op jit(solution)/shard_map/ppermute | solution.py:39
  64.1 8.7 %collective-permute-start.15 = (bf16[2,192,512]{2,1,0:T(8,128)(2,1)S(1)}, bf16[2,192,512]{2,1,0:T(8,128)(2,1)S(1)}, u32[]{:S(2)}, u32[]{:S(2)}) collective-permute-start(bf16[2,192,512]{2,1,0:T(8,128)(2,1)S(1)} %collective-permute-done.8.refs_4_), channel_id=1, source_target_pairs={{0,16},{16,0},{32,48},{48,32},{64,80},{80,64},{96,112},{112,96},{1... | collective-permute-start | bytes 1179656 | tf_op jit(solution)/shard_map/ppermute | solution.py:39
  64.1 8.7 %collective-permute-start.9 = (bf16[2,192,512]{2,1,0:T(8,128)(2,1)S(1)}, bf16[2,192,512]{2,1,0:T(8,128)(2,1)S(1)}, u32[]{:S(2)}, u32[]{:S(2)}) collective-permute-start(bf16[2,192,512]{2,1,0:T(8,128)(2,1)S(1)} %pad_maximum_fusion.1.refs_0_), channel_id=1, source_target_pairs={{0,16},{16,0},{32,48},{48,32},{64,80},{80,64},{96,112},{112,96},{1... | collective-permute-start | bytes 1179656 | tf_op jit(solution)/shard_map/ppermute | solution.py:39
  84.6 7.8 %collective-permute-start.17 = (bf16[128,256]{1,0:T(8,128)(2,1)S(1)}, bf16[128,256]{1,0:T(8,128)(2,1)S(1)}, u32[]{:S(2)}, u32[]{:S(2)}) collective-permute-start(bf16[128,256]{1,0:T(8,128)(2,1)S(1)} %attend.2.refs_0_), channel_id=1, source_target_pairs={{0,4},{1,5},{2,6},{3,7},{4,8},{5,9},{6,10},{7,11},{8,12},{9,13},{1... | collective-permute-start | bytes 196616 | tf_op jit(solution)/shard_map/ppermute | solution.py:28
  86.7 6.9 %collective-permute-start.18 = (bf16[128,256]{1,0:T(8,128)(2,1)S(1)}, bf16[128,256]{1,0:T(8,128)(2,1)S(1)}, u32[]{:S(2)}, u32[]{:S(2)}) collective-permute-start(bf16[128,256]{1,0:T(8,128)(2,1)S(1)} %attend.2.refs_0_), channel_id=1, source_target_pairs={{0,8},{1,9},{2,10},{3,11},{4,12},{5,13},{6,14},{7,15},{8,0},{9,1},... | collective-permute-start | bytes 196616 | tf_op jit(solution)/shard_map/ppermute | solution.py:28
  94.5 6.4 %collective-permute-start.20 = (bf16[192,256]{1,0:T(8,128)(2,1)S(1)}, bf16[192,256]{1,0:T(8,128)(2,1)S(1)}, u32[]{:S(2)}, u32[]{:S(2)}) collective-permute-start(bf16[192,256]{1,0:T(8,128)(2,1)S(1)} %get-tuple-element.78), channel_id=1, source_target_pairs={{0,1},{1,2},{2,3},{3,0},{4,5},{5,6},{6,7},{7,4},{8,9},{9,10},{10,1... | collective-permute-start | bytes 294920 | tf_op jit(solution)/shard_map/ppermute | solution.py:28
  97.3 6.2 %collective-permute-start.21 = (bf16[192,256]{1,0:T(8,128)(2,1)S(1)}, bf16[192,256]{1,0:T(8,128)(2,1)S(1)}, u32[]{:S(2)}, u32[]{:S(2)}) collective-permute-start(bf16[192,256]{1,0:T(8,128)(2,1)S(1)} %get-tuple-element.79), channel_id=1, source_target_pairs={{0,2},{1,3},{2,0},{3,1},{4,6},{5,7},{6,4},{7,5},{8,10},{9,11},{10,... | collective-permute-start | bytes 294920 | tf_op jit(solution)/shard_map/ppermute | solution.py:28
  98.3 6.3 %collective-permute-start.22 = (bf16[192,256]{1,0:T(8,128)(2,1)S(1)}, bf16[192,256]{1,0:T(8,128)(2,1)S(1)}, u32[]{:S(2)}, u32[]{:S(2)}) collective-permute-start(bf16[192,256]{1,0:T(8,128)(2,1)S(1)} %get-tuple-element.80), channel_id=1, source_target_pairs={{0,3},{1,0},{2,1},{3,2},{4,7},{5,4},{6,5},{7,6},{8,11},{9,8},{10,9... | collective-permute-start | bytes 294920 | tf_op jit(solution)/shard_map/ppermute | solution.py:28
  105.4 7.6 %collective-permute-start.23 = (bf16[192,256]{1,0:T(8,128)(2,1)S(1)}, bf16[192,256]{1,0:T(8,128)(2,1)S(1)}, u32[]{:S(2)}, u32[]{:S(2)}) collective-permute-start(bf16[192,256]{1,0:T(8,128)(2,1)S(1)} %update.2.x), channel_id=1, source_target_pairs={{0,4},{1,5},{2,6},{3,7},{4,8},{5,9},{6,10},{7,11},{8,12},{9,13},{1... | collective-permute-start | bytes 294920 | tf_op jit(solution)/shard_map/ppermute | solution.py:28
  107.4 8.2 %collective-permute-start.24 = (bf16[192,256]{1,0:T(8,128)(2,1)S(1)}, bf16[192,256]{1,0:T(8,128)(2,1)S(1)}, u32[]{:S(2)}, u32[]{:S(2)}) collective-permute-start(bf16[192,256]{1,0:T(8,128)(2,1)S(1)} %update.2.x), channel_id=1, source_target_pairs={{0,8},{1,9},{2,10},{3,11},{4,12},{5,13},{6,14},{7,15},{8,0},{9,1},... | collective-permute-start | bytes 294920 | tf_op jit(solution)/shard_map/ppermute | solution.py:28
  115.7 12.3 %collective-permute-start.26 = (bf16[4,192,256]{2,1,0:T(8,128)(2,1)S(1)}, bf16[4,192,256]{2,1,0:T(8,128)(2,1)S(1)}, u32[]{:S(2)}, u32[]{:S(2)}) collective-permute-start(bf16[4,192,256]{2,1,0:T(8,128)(2,1)S(1)} %pad_maximum_fusion.2.refs_0_), channel_id=1, source_target_pairs={{0,1},{1,2},{2,3},{3,0},{4,5},{5,6},{6,7},{7,4},{8,9},{9,10},{10,1... | collective-permute-start | bytes 1179656 | tf_op jit(solution)/shard_map/ppermute | solution.py:28
  116.1 13.6 %collective-permute-start.27 = (bf16[4,192,256]{2,1,0:T(8,128)(2,1)S(1)}, bf16[4,192,256]{2,1,0:T(8,128)(2,1)S(1)}, u32[]{:S(2)}, u32[]{:S(2)}) collective-permute-start(bf16[4,192,256]{2,1,0:T(8,128)(2,1)S(1)} %pad_maximum_fusion.2.refs_0_), channel_id=1, source_target_pairs={{0,2},{1,3},{2,0},{3,1},{4,6},{5,7},{6,4},{7,5},{8,10},{9,11},{10,... | collective-permute-start | bytes 1179656 | tf_op jit(solution)/shard_map/ppermute | solution.py:28
  118.3 18.5 %collective-permute-start.28 = (bf16[4,192,256]{2,1,0:T(8,128)(2,1)S(1)}, bf16[4,192,256]{2,1,0:T(8,128)(2,1)S(1)}, u32[]{:S(2)}, u32[]{:S(2)}) collective-permute-start(bf16[4,192,256]{2,1,0:T(8,128)(2,1)S(1)} %pad_maximum_fusion.2.refs_0_), channel_id=1, source_target_pairs={{0,3},{1,0},{2,1},{3,2},{4,7},{5,4},{6,5},{7,6},{8,11},{9,8},{10,9... | collective-permute-start | bytes 1179656 | tf_op jit(solution)/shard_map/ppermute | solution.py:28
  150.3 6.9 %collective-permute-start.29 = (bf16[128,256]{1,0:T(8,128)(2,1)S(1)}, bf16[128,256]{1,0:T(8,128)(2,1)S(1)}, u32[]{:S(2)}, u32[]{:S(2)}) collective-permute-start(bf16[128,256]{1,0:T(8,128)(2,1)S(1)} %attend.3.refs_0_), channel_id=1, source_target_pairs={{0,4},{1,5},{2,6},{3,7},{4,8},{5,9},{6,10},{7,11},{8,12},{9,13},{1... | collective-permute-start | bytes 196616 | tf_op jit(solution)/shard_map/ppermute | solution.py:28
  151.0 8.3 %collective-permute-start.30 = (bf16[128,256]{1,0:T(8,128)(2,1)S(1)}, bf16[128,256]{1,0:T(8,128)(2,1)S(1)}, u32[]{:S(2)}, u32[]{:S(2)}) collective-permute-start(bf16[128,256]{1,0:T(8,128)(2,1)S(1)} %attend.3.refs_0_), channel_id=1, source_target_pairs={{0,8},{1,9},{2,10},{3,11},{4,12},{5,13},{6,14},{7,15},{8,0},{9,1},... | collective-permute-start | bytes 196616 | tf_op jit(solution)/shard_map/ppermute | solution.py:28
  151.0 8.3 %collective-permute-start.31 = (bf16[128,256]{1,0:T(8,128)(2,1)S(1)}, bf16[128,256]{1,0:T(8,128)(2,1)S(1)}, u32[]{:S(2)}, u32[]{:S(2)}) collective-permute-start(bf16[128,256]{1,0:T(8,128)(2,1)S(1)} %attend.3.refs_0_), channel_id=1, source_target_pairs={{0,12},{1,13},{2,14},{3,15},{4,0},{5,1},{6,2},{7,3},{8,4},{9,5},{1... | collective-permute-start | bytes 196616 | tf_op jit(solution)/shard_map/ppermute | solution.py:28
  160.9 6.5 %collective-permute-start.33 = (bf16[192,256]{1,0:T(8,128)(2,1)S(1)}, bf16[192,256]{1,0:T(8,128)(2,1)S(1)}, u32[]{:S(2)}, u32[]{:S(2)}) collective-permute-start(bf16[192,256]{1,0:T(8,128)(2,1)S(1)} %get-tuple-element.89), channel_id=1, source_target_pairs={{0,2},{1,3},{2,0},{3,1},{4,6},{5,7},{6,4},{7,5},{8,10},{9,11},{10,... | collective-permute-start | bytes 294920 | tf_op jit(solution)/shard_map/ppermute | solution.py:28
  (19 other events, 137.8 us)
Sparse Core Ops, SparseCore 0:
  10.7 69.8 all-gather.3
  83.2 62.0 all-gather.5

commit v2 on v1

--- a/solution.py
+++ b/solution.py
@@ -234,8 +234,9 @@
     w_up, w_down, w_pair = sync(w_up, w_down, w_pair)
     w_far = [shift(w_up[:1], "y", 1), shift(w_down[1:], "y", 3)]
     w_quad = [w_pair, w_up, *w_far, w_down]
-    w_c = [shift(piece, "c", 1) for piece in w_quad]
     normed = norm(0, [x_four, x_up, x_far, x_down])
+    ready = [w_pair, w_up, *(sync(piece, normed)[0] for piece in w_far), w_down]
+    w_c = [shift(piece, "c", 1) for piece in ready]
     w_c, w_quad, normed = sync(w_c, w_quad, normed)
     past = cache_all
     weights = w_quad + w_c

time: 178 us -> 186 us (1.045)
  the two profiles are of different devices: /device:TPU:6 before, /device:TPU:224 now
where the time goes in v2:
time: 186 us
  waiting for transfers between devices  74 us (40%)
  starting transfers between devices  69.1 us (37%)
  Pallas kernels  19.6 us (11%)
  between operations  14.3 us (8%)
  local copies, waits for them, and re-layouts  7.87 us (4%)
    ppermute x24, starting transfers between devices, shift(): return lax.ppermute(array, 'tp', pairs)  47.8 us
    ppermute x24, waiting for transfers between devices, shift(): return lax.ppermute(array, 'tp', pairs)  41.5 us
    ppermute x10, waiting for transfers between devices, shift(): return lax.ppermute(array, 'patch', pairs)  25.3 us
    pallas_call x11, Pallas kernels, call(): pl.pallas_call(body, out_shape=outs, in_specs=[pl.BlockSpec(memory_space=...  19.6 us
    ppermute x10, starting transfers between devices, shift(): return lax.ppermute(array, 'patch', pairs)  7.92 us
    all_to_all x1, starting transfers between devices, on_device(): w_mine = lax.all_to_all(sent, 'tp', 0, 0)  7.58 us
    ppermute x1, waiting for transfers between devices, swap(): return lax.ppermute(array, ('patch', 'tp'), pairs)  6.51 us
    unnamed x28, local copies, waits for them, and re-layouts  5.76 us
  transfers between devices with their start and end apart: 38, of which 19 were waited for; matrix products, arithmetic and copies ran while one was open for 2% of the time, Pallas kernels for 8%

profile of v2, /device:TPU:224, one launch (start us, length us, event | category | flops | bytes accessed | tf_op | source)
XLA Modules:
  0.0 186.0 jit_solution(7887461548272368123)
XLA Ops:
  9.7 7.6 %all-to-all-start = ((bf16[16,36,128]{2,1,0:T(8,128)(2,1)}), bf16[16,36,128]{2,1,0:T(8,128)(2,1)S(1)}, u32[]{:S(2)}, u32[]{:S(2)}) async-start(bf16[16,36,128]{2,1,0:T(8,128)(2,1)} %copy.14), calls=%async_computation | async-start | bytes 327680 | tf_op jit(solution)/shard_map/all_to_all | solution.py:220
  17.5 1.9 %collective-permute-start.1 = (bf16[192,256]{1,0:T(8,128)(2,1)}, bf16[192,256]{1,0:T(8,128)(2,1)S(1)}, u32[]{:S(2)}, u32[]{:S(2)}) collective-permute-start(bf16[192,256]{1,0:T(8,128)(2,1)} %bitcast.32), channel_id=1, source_target_pairs={{0,8},{1,9},{2,10},{3,11},{4,12},{5,13},{6,14},{7,15},{8,0},{9,1},... | collective-permute-start | bytes 294920 | tf_op jit(solution)/shard_map/ppermute | solution.py:28
  20.0 5.7 %collective-permute-start.3 = (bf16[192,128]{1,0:T(8,128)(2,1)}, bf16[192,128]{1,0:T(8,128)(2,1)S(1)}, u32[]{:S(2)}, u32[]{:S(2)}) collective-permute-start(bf16[192,128]{1,0:T(8,128)(2,1)} %param.11), channel_id=1, source_target_pairs={{0,0},{1,16},{2,32},{3,48},{4,4},{5,20},{6,36},{7,52},{8,8},{9,24}... | collective-permute-start | bytes 147464 | tf_op jit(solution)/shard_map/ppermute | solution.py:192
  26.9 6.5 %collective-permute-done.3 = bf16[192,128]{1,0:T(8,128)(2,1)S(1)} collective-permute-done((bf16[192,128]{1,0:T(8,128)(2,1)}, bf16[192,128]{1,0:T(8,128)(2,1)S(1)}, u32[]{:S(2)}, u32[]{:S(2)}) %collective-permute-start.3) | collective-permute-done | bytes 49184 | tf_op jit(solution)/shard_map/ppermute | solution.py:192
  38.9 10.0 %collective-permute-done.4 = bf16[192,512]{1,0:T(8,128)(2,1)S(1)} collective-permute-done((bf16[192,512]{1,0:T(8,128)(2,1)S(1)}, bf16[192,512]{1,0:T(8,128)(2,1)S(1)}, u32[]{:S(2)}, u32[]{:S(2)}) %collective-permute-start.4) | collective-permute-done | bytes 196640 | tf_op jit(solution)/shard_map/ppermute | solution.py:39
  54.1 8.0 %collective-permute-done.7.refs_1_ = bf16[2,192,512]{2,1,0:T(8,128)(2,1)S(1)} collective-permute-done((bf16[2,192,512]{2,1,0:T(8,128)(2,1)S(1)}, bf16[2,192,512]{2,1,0:T(8,128)(2,1)S(1)}, u32[]{:S(2)}, u32[]{:S(2)}) %collective-permute-start.7) | collective-permute-done | bytes 393248 | tf_op jit(solution)/shard_map/ppermute | solution.py:39
  62.2 3.3 %collective-permute-start.14 = (bf16[1,192,512]{2,1,0:T(8,128)(2,1)S(1)}, bf16[1,192,512]{2,1,0:T(8,128)(2,1)S(1)}, u32[]{:S(2)}, u32[]{:S(2)}) collective-permute-start(bf16[1,192,512]{2,1,0:T(8,128)(2,1)S(1)} %slice.7), channel_id=1, source_target_pairs={{0,192},{16,208},{32,224},{48,240},{64,0},{80,16},{96,32},{112,48}... | collective-permute-start | bytes 589832 | tf_op jit(solution)/shard_map/ppermute | solution.py:39
  66.3 2.2 %norm.2.normed = bf16[16,192,256]{2,1,0:T(8,128)(2,1)S(1)} custom-call(s32[2]{0:T(128)S(1)} %pad_add_fusion.ids, f32[96,192]{1,0:T(8,128)S(1)} %reshape.30.mod, bf16[4,192,256]{2,1,0:T(8,128)(2,1)S(1)} %pad_maximum_fusion.refs_0_, bf16[4,192,256]{2,1,0:T(8,128)(2,1)S(1)} %collective-permute-done.5.refs_1_, ...), custom_call_target="tpu_custom_call" | custom-call | flops 1048576 | bytes 4194304 | tf_op jit(solution)/shard_map/norm/pallas_call | solution.py:53
  68.5 1.9 %collective-permute-done.14.refs_3_ = bf16[1,192,512]{2,1,0:T(8,128)(2,1)S(1)} collective-permute-done((bf16[1,192,512]{2,1,0:T(8,128)(2,1)S(1)}, bf16[1,192,512]{2,1,0:T(8,128)(2,1)S(1)}, u32[]{:S(2)}, u32[]{:S(2)}) %collective-permute-start.14) | collective-permute-done | bytes 196640 | tf_op jit(solution)/shard_map/ppermute | solution.py:39
  70.4 3.9 %collective-permute-done.11.refs_2_ = bf16[1,192,512]{2,1,0:T(8,128)(2,1)S(1)} collective-permute-done((bf16[1,192,512]{2,1,0:T(8,128)(2,1)S(1)}, bf16[1,192,512]{2,1,0:T(8,128)(2,1)S(1)}, u32[]{:S(2)}, u32[]{:S(2)}) %collective-permute-start.11) | collective-permute-done | bytes 196640 | tf_op jit(solution)/shard_map/ppermute | solution.py:39
  75.8 2.7 %qkv.2 = (bf16[512,128]{1,0:T(8,128)(2,1)}, bf16[768,128]{1,0:T(8,128)(2,1)S(1)}) custom-call(s32[2]{0:T(128)S(1)} %pad_add_fusion.ids, bf16[16,192,256]{2,1,0:T(8,128)(2,1)S(1)} %norm.2.normed, f32[1,128]{1,0:T(1,128)S(1)} %bitcast.36, f32[1,128]{1,0:T(1,128)S(1)} %bitcast.38, bf16[2,192,512]{2,1,0:T(8,128)(2,1)S(1)} %pad_maximum_fusion.1.refs_0_, ...), custom_call_target="tpu_custom_call" | custom-call | flops 1048576 | bytes 16777216 | tf_op jit(solution)/shard_map/qkv/pallas_call | solution.py:53
  80.1 2.4 %attend.2.refs_0_ = bf16[128,256]{1,0:T(8,128)(2,1)S(1)} custom-call(s32[2]{0:T(128)S(1)} %pad_add_fusion.ids, bf16[768,128]{1,0:T(8,128)(2,1)S(1)} %get-tuple-element.76.near, bf16[16,512,128]{2,1,0:T(8,128)(2,1)S(1)} %copy-done), custom_call_target="tpu_custom_call" | custom-call | flops 1048576 | bytes 8388608 | tf_op jit(solution)/shard_map/attend/pallas_call | solution.py:53
  82.5 3.2 %collective-permute-start.17 = (bf16[128,256]{1,0:T(8,128)(2,1)S(1)}, bf16[128,256]{1,0:T(8,128)(2,1)S(1)}, u32[]{:S(2)}, u32[]{:S(2)}) collective-permute-start(bf16[128,256]{1,0:T(8,128)(2,1)S(1)} %attend.2.refs_0_), channel_id=1, source_target_pairs={{0,4},{1,5},{2,6},{3,7},{4,8},{5,9},{6,10},{7,11},{8,12},{9,13},{1... | collective-permute-start | bytes 196616 | tf_op jit(solution)/shard_map/ppermute | solution.py:28
  85.8 1.8 collective-permute-start.18
  90.3 6.5 %collective-permute-done.18.refs_2_ = bf16[128,256]{1,0:T(8,128)(2,1)S(1)} collective-permute-done((bf16[128,256]{1,0:T(8,128)(2,1)S(1)}, bf16[128,256]{1,0:T(8,128)(2,1)S(1)}, u32[]{:S(2)}, u32[]{:S(2)}) %collective-permute-start.18) | collective-permute-done | bytes 65568 | tf_op jit(solution)/shard_map/ppermute | solution.py:28
  97.9 3.1 %collective-permute-start.22 = (bf16[192,256]{1,0:T(8,128)(2,1)S(1)}, bf16[192,256]{1,0:T(8,128)(2,1)S(1)}, u32[]{:S(2)}, u32[]{:S(2)}) collective-permute-start(bf16[192,256]{1,0:T(8,128)(2,1)S(1)} %get-tuple-element.84), channel_id=1, source_target_pairs={{0,3},{1,0},{2,1},{3,2},{4,7},{5,4},{6,5},{7,6},{8,11},{9,8},{10,9... | collective-permute-start | bytes 294920 | tf_op jit(solution)/shard_map/ppermute | solution.py:28
  101.1 3.6 %collective-permute-done.20.refs_0_ = bf16[192,256]{1,0:T(8,128)(2,1)S(1)} collective-permute-done((bf16[192,256]{1,0:T(8,128)(2,1)S(1)}, bf16[192,256]{1,0:T(8,128)(2,1)S(1)}, u32[]{:S(2)}, u32[]{:S(2)}) %collective-permute-start.20) | collective-permute-done | bytes 98336 | tf_op jit(solution)/shard_map/ppermute | solution.py:28
  108.3 1.9 %collective-permute-start.25 = (bf16[192,256]{1,0:T(8,128)(2,1)S(1)}, bf16[192,256]{1,0:T(8,128)(2,1)S(1)}, u32[]{:S(2)}, u32[]{:S(2)}) collective-permute-start(bf16[192,256]{1,0:T(8,128)(2,1)S(1)} %update.2.x), channel_id=1, source_target_pairs={{0,12},{1,13},{2,14},{3,15},{4,0},{5,1},{6,2},{7,3},{8,4},{9,5},{1... | collective-permute-start | bytes 294920 | tf_op jit(solution)/shard_map/ppermute | solution.py:28
  111.2 5.3 %collective-permute-done.24 = bf16[192,256]{1,0:T(8,128)(2,1)S(1)} collective-permute-done((bf16[192,256]{1,0:T(8,128)(2,1)S(1)}, bf16[192,256]{1,0:T(8,128)(2,1)S(1)}, u32[]{:S(2)}, u32[]{:S(2)}) %collective-permute-start.24) | collective-permute-done | bytes 98336 | tf_op jit(solution)/shard_map/ppermute | solution.py:28
  117.4 3.8 %collective-permute-start.27 = (bf16[4,192,256]{2,1,0:T(8,128)(2,1)S(1)}, bf16[4,192,256]{2,1,0:T(8,128)(2,1)S(1)}, u32[]{:S(2)}, u32[]{:S(2)}) collective-permute-start(bf16[4,192,256]{2,1,0:T(8,128)(2,1)S(1)} %pad_maximum_fusion.2.refs_0_), channel_id=1, source_target_pairs={{0,2},{1,3},{2,0},{3,1},{4,6},{5,7},{6,4},{7,5},{8,10},{9,11},{10,... | collective-permute-start | bytes 1179656 | tf_op jit(solution)/shard_map/ppermute | solution.py:28
  121.2 7.7 %collective-permute-done.26.refs_1_ = bf16[4,192,256]{2,1,0:T(8,128)(2,1)S(1)} collective-permute-done((bf16[4,192,256]{2,1,0:T(8,128)(2,1)S(1)}, bf16[4,192,256]{2,1,0:T(8,128)(2,1)S(1)}, u32[]{:S(2)}, u32[]{:S(2)}) %collective-permute-start.26) | collective-permute-done | bytes 393248 | tf_op jit(solution)/shard_map/ppermute | solution.py:28
  128.8 7.1 %collective-permute-done.27.refs_2_ = bf16[4,192,256]{2,1,0:T(8,128)(2,1)S(1)} collective-permute-done((bf16[4,192,256]{2,1,0:T(8,128)(2,1)S(1)}, bf16[4,192,256]{2,1,0:T(8,128)(2,1)S(1)}, u32[]{:S(2)}, u32[]{:S(2)}) %collective-permute-start.27) | collective-permute-done | bytes 393248 | tf_op jit(solution)/shard_map/ppermute | solution.py:28
  136.0 2.2 %norm.3.normed = bf16[16,192,256]{2,1,0:T(8,128)(2,1)S(1)} custom-call(s32[2]{0:T(128)S(1)} %pad_add_fusion.ids, f32[96,192]{1,0:T(8,128)S(1)} %reshape.30.mod, bf16[4,192,256]{2,1,0:T(8,128)(2,1)S(1)} %pad_maximum_fusion.2.refs_0_, bf16[4,192,256]{2,1,0:T(8,128)(2,1)S(1)} %collective-permute-done.26.refs_1_, ...), custom_call_target="tpu_custom_call" | custom-call | flops 1048576 | bytes 4194304 | tf_op jit(solution)/shard_map/norm/pallas_call | solution.py:53
  138.2 2.7 %qkv.3 = (bf16[512,128]{1,0:T(8,128)(2,1)}, bf16[768,128]{1,0:T(8,128)(2,1)S(1)}) custom-call(s32[2]{0:T(128)S(1)} %pad_add_fusion.ids, bf16[16,192,256]{2,1,0:T(8,128)(2,1)S(1)} %norm.3.normed, f32[1,128]{1,0:T(1,128)S(1)} %bitcast.37, f32[1,128]{1,0:T(1,128)S(1)} %bitcast.39, bf16[2,192,512]{2,1,0:T(8,128)(2,1)S(1)} %pad_maximum_fusion.1.refs_0_, ...), custom_call_target="tpu_custom_call" | custom-call | flops 1048576 | bytes 16777216 | tf_op jit(solution)/shard_map/qkv/pallas_call | solution.py:53
  144.1 2.4 %attend.3.refs_0_ = bf16[128,256]{1,0:T(8,128)(2,1)S(1)} custom-call(s32[2]{0:T(128)S(1)} %pad_add_fusion.ids, bf16[768,128]{1,0:T(8,128)(2,1)S(1)} %copy-done.10, bf16[16,512,128]{2,1,0:T(8,128)(2,1)S(1)} %bitcast.29), custom_call_target="tpu_custom_call" | custom-call | flops 1048576 | bytes 8388608 | tf_op jit(solution)/shard_map/attend/pallas_call | solution.py:53
  146.5 3.2 %collective-permute-start.29 = (bf16[128,256]{1,0:T(8,128)(2,1)S(1)}, bf16[128,256]{1,0:T(8,128)(2,1)S(1)}, u32[]{:S(2)}, u32[]{:S(2)}) collective-permute-start(bf16[128,256]{1,0:T(8,128)(2,1)S(1)} %attend.3.refs_0_), channel_id=1, source_target_pairs={{0,4},{1,5},{2,6},{3,7},{4,8},{5,9},{6,10},{7,11},{8,12},{9,13},{1... | collective-permute-start | bytes 196616 | tf_op jit(solution)/shard_map/ppermute | solution.py:28
  149.7 12.4 %collective-permute-start.30 = (bf16[128,256]{1,0:T(8,128)(2,1)S(1)}, bf16[128,256]{1,0:T(8,128)(2,1)S(1)}, u32[]{:S(2)}, u32[]{:S(2)}) collective-permute-start(bf16[128,256]{1,0:T(8,128)(2,1)S(1)} %attend.3.refs_0_), channel_id=1, source_target_pairs={{0,8},{1,9},{2,10},{3,11},{4,12},{5,13},{6,14},{7,15},{8,0},{9,1},... | collective-permute-start | bytes 196616 | tf_op jit(solution)/shard_map/ppermute | solution.py:28
  162.1 1.9 %collective-permute-start.31 = (bf16[128,256]{1,0:T(8,128)(2,1)S(1)}, bf16[128,256]{1,0:T(8,128)(2,1)S(1)}, u32[]{:S(2)}, u32[]{:S(2)}) collective-permute-start(bf16[128,256]{1,0:T(8,128)(2,1)S(1)} %attend.3.refs_0_), channel_id=1, source_target_pairs={{0,12},{1,13},{2,14},{3,15},{4,0},{5,1},{6,2},{7,3},{8,4},{9,5},{1... | collective-permute-start | bytes 196616 | tf_op jit(solution)/shard_map/ppermute | solution.py:28
  164.1 2.0 %collective-permute-done.30.refs_2_ = bf16[128,256]{1,0:T(8,128)(2,1)S(1)} collective-permute-done((bf16[128,256]{1,0:T(8,128)(2,1)S(1)}, bf16[128,256]{1,0:T(8,128)(2,1)S(1)}, u32[]{:S(2)}, u32[]{:S(2)}) %collective-permute-start.30) | collective-permute-done | bytes 65568 | tf_op jit(solution)/shard_map/ppermute | solution.py:28
  166.0 2.2 %collective-permute-done.31.refs_3_ = bf16[128,256]{1,0:T(8,128)(2,1)S(1)} collective-permute-done((bf16[128,256]{1,0:T(8,128)(2,1)S(1)}, bf16[128,256]{1,0:T(8,128)(2,1)S(1)}, u32[]{:S(2)}, u32[]{:S(2)}) %collective-permute-start.31) | collective-permute-done | bytes 65568 | tf_op jit(solution)/shard_map/ppermute | solution.py:28
  169.3 3.9 %collective-permute-start.33 = (bf16[192,256]{1,0:T(8,128)(2,1)S(1)}, bf16[192,256]{1,0:T(8,128)(2,1)S(1)}, u32[]{:S(2)}, u32[]{:S(2)}) collective-permute-start(bf16[192,256]{1,0:T(8,128)(2,1)S(1)} %get-tuple-element.93), channel_id=1, source_target_pairs={{0,2},{1,3},{2,0},{3,1},{4,6},{5,7},{6,4},{7,5},{8,10},{9,11},{10,... | collective-permute-start | bytes 294920 | tf_op jit(solution)/shard_map/ppermute | solution.py:28
  173.1 2.9 %collective-permute-done.32.refs_0_ = bf16[192,256]{1,0:T(8,128)(2,1)S(1)} collective-permute-done((bf16[192,256]{1,0:T(8,128)(2,1)S(1)}, bf16[192,256]{1,0:T(8,128)(2,1)S(1)}, u32[]{:S(2)}, u32[]{:S(2)}) %collective-permute-start.32) | collective-permute-done | bytes 98336 | tf_op jit(solution)/shard_map/ppermute | solution.py:28
  (98 shorter events, 35.6 us)
Async XLA Ops:
  7.2 71.3 %all-gather.4.cloned.1.call-start = ((), (), s32[]{:S(2)}) async-start(), calls=%async_computation.1 | async-start | bytes 2228224 | tf_op jit(solution)/shard_map/all_gather | solution.py:222
  9.7 24.2 %all-to-all-start = ((bf16[16,36,128]{2,1,0:T(8,128)(2,1)}), bf16[16,36,128]{2,1,0:T(8,128)(2,1)S(1)}, u32[]{:S(2)}, u32[]{:S(2)}) async-start(bf16[16,36,128]{2,1,0:T(8,128)(2,1)} %copy.14), calls=%async_computation | async-start | bytes 327680 | tf_op jit(solution)/shard_map/all_to_all | solution.py:220
  17.3 124.3 %all-gather.6.cloned.1.call-start = ((), (), s32[]{:S(2)}) async-start(), calls=%async_computation.2 | async-start | bytes 2228224 | tf_op jit(solution)/shard_map/all_gather | solution.py:256
  17.3 16.0 %collective-permute-start = (bf16[192,256]{1,0:T(8,128)(2,1)}, bf16[192,256]{1,0:T(8,128)(2,1)S(1)}, u32[]{:S(2)}, u32[]{:S(2)}) collective-permute-start(bf16[192,256]{1,0:T(8,128)(2,1)} %bitcast.31), channel_id=1, source_target_pairs={{0,4},{1,5},{2,6},{3,7},{4,8},{5,9},{6,10},{7,11},{8,12},{9,13},{1... | collective-permute-start | bytes 294920 | tf_op jit(solution)/shard_map/ppermute | solution.py:28
  17.5 16.4 %collective-permute-start.1 = (bf16[192,256]{1,0:T(8,128)(2,1)}, bf16[192,256]{1,0:T(8,128)(2,1)S(1)}, u32[]{:S(2)}, u32[]{:S(2)}) collective-permute-start(bf16[192,256]{1,0:T(8,128)(2,1)} %bitcast.32), channel_id=1, source_target_pairs={{0,8},{1,9},{2,10},{3,11},{4,12},{5,13},{6,14},{7,15},{8,0},{9,1},... | collective-permute-start | bytes 294920 | tf_op jit(solution)/shard_map/ppermute | solution.py:28
  19.4 14.5 %collective-permute-start.2 = (bf16[192,256]{1,0:T(8,128)(2,1)}, bf16[192,256]{1,0:T(8,128)(2,1)S(1)}, u32[]{:S(2)}, u32[]{:S(2)}) collective-permute-start(bf16[192,256]{1,0:T(8,128)(2,1)} %bitcast.33), channel_id=1, source_target_pairs={{0,12},{1,13},{2,14},{3,15},{4,0},{5,1},{6,2},{7,3},{8,4},{9,5},{1... | collective-permute-start | bytes 294920 | tf_op jit(solution)/shard_map/ppermute | solution.py:28
  20.0 13.4 %collective-permute-start.3 = (bf16[192,128]{1,0:T(8,128)(2,1)}, bf16[192,128]{1,0:T(8,128)(2,1)S(1)}, u32[]{:S(2)}, u32[]{:S(2)}) collective-permute-start(bf16[192,128]{1,0:T(8,128)(2,1)} %param.11), channel_id=1, source_target_pairs={{0,0},{1,16},{2,32},{3,48},{4,4},{5,20},{6,36},{7,52},{8,8},{9,24}... | collective-permute-start | bytes 147464 | tf_op jit(solution)/shard_map/ppermute | solution.py:192
  34.9 14.1 %collective-permute-start.5 = (bf16[4,192,256]{2,1,0:T(8,128)(2,1)S(1)}, bf16[4,192,256]{2,1,0:T(8,128)(2,1)S(1)}, u32[]{:S(2)}, u32[]{:S(2)}) collective-permute-start(bf16[4,192,256]{2,1,0:T(8,128)(2,1)S(1)} %pad_maximum_fusion.refs_0_), channel_id=1, source_target_pairs={{0,1},{1,2},{2,3},{3,0},{4,5},{5,6},{6,7},{7,4},{8,9},{9,10},{10,1... | collective-permute-start | bytes 1179656 | tf_op jit(solution)/shard_map/ppermute | solution.py:28
  36.5 12.5 %collective-permute-start.6 = (bf16[4,192,256]{2,1,0:T(8,128)(2,1)S(1)}, bf16[4,192,256]{2,1,0:T(8,128)(2,1)S(1)}, u32[]{:S(2)}, u32[]{:S(2)}) collective-permute-start(bf16[4,192,256]{2,1,0:T(8,128)(2,1)S(1)} %pad_maximum_fusion.refs_0_), channel_id=1, source_target_pairs={{0,3},{1,0},{2,1},{3,2},{4,7},{5,4},{6,5},{7,6},{8,11},{9,8},{10,9... | collective-permute-start | bytes 1179656 | tf_op jit(solution)/shard_map/ppermute | solution.py:28
  38.4 10.6 %collective-permute-start.4 = (bf16[192,512]{1,0:T(8,128)(2,1)S(1)}, bf16[192,512]{1,0:T(8,128)(2,1)S(1)}, u32[]{:S(2)}, u32[]{:S(2)}) collective-permute-start(bf16[192,512]{1,0:T(8,128)(2,1)S(1)} %constant_dynamic-update-slice_fusion), channel_id=1, source_target_pairs={{0,32},{16,48},{32,0},{48,16},{64,96},{80,112},{96,64},{112,80},{1... | collective-permute-start | bytes 589832 | tf_op jit(solution)/shard_map/ppermute | solution.py:39
  49.1 13.1 %collective-permute-start.7 = (bf16[2,192,512]{2,1,0:T(8,128)(2,1)S(1)}, bf16[2,192,512]{2,1,0:T(8,128)(2,1)S(1)}, u32[]{:S(2)}, u32[]{:S(2)}) collective-permute-start(bf16[2,192,512]{2,1,0:T(8,128)(2,1)S(1)} %pad_maximum_fusion.1.refs_0_), channel_id=1, source_target_pairs={{0,64},{16,80},{32,96},{48,112},{64,128},{80,144},{96,160},{112,17... | collective-permute-start | bytes 1179656 | tf_op jit(solution)/shard_map/ppermute | solution.py:39
  50.8 11.4 %collective-permute-start.8 = (bf16[2,192,512]{2,1,0:T(8,128)(2,1)S(1)}, bf16[2,192,512]{2,1,0:T(8,128)(2,1)S(1)}, u32[]{:S(2)}, u32[]{:S(2)}) collective-permute-start(bf16[2,192,512]{2,1,0:T(8,128)(2,1)S(1)} %pad_maximum_fusion.1.refs_0_), channel_id=1, source_target_pairs={{0,192},{16,208},{32,224},{48,240},{64,0},{80,16},{96,32},{112,48}... | collective-permute-start | bytes 1179656 | tf_op jit(solution)/shard_map/ppermute | solution.py:39
  52.4 13.8 %collective-permute-start.12 = (bf16[4,192,256]{2,1,0:T(8,128)(2,1)S(1)}, bf16[4,192,256]{2,1,0:T(8,128)(2,1)S(1)}, u32[]{:S(2)}, u32[]{:S(2)}) collective-permute-start(bf16[4,192,256]{2,1,0:T(8,128)(2,1)S(1)} %pad_maximum_fusion.refs_0_), channel_id=1, source_target_pairs={{0,2},{1,3},{2,0},{3,1},{4,6},{5,7},{6,4},{7,5},{8,10},{9,11},{10,... | collective-permute-start | bytes 1179656 | tf_op jit(solution)/shard_map/ppermute | solution.py:28
  62.2 8.3 %collective-permute-start.14 = (bf16[1,192,512]{2,1,0:T(8,128)(2,1)S(1)}, bf16[1,192,512]{2,1,0:T(8,128)(2,1)S(1)}, u32[]{:S(2)}, u32[]{:S(2)}) collective-permute-start(bf16[1,192,512]{2,1,0:T(8,128)(2,1)S(1)} %slice.7), channel_id=1, source_target_pairs={{0,192},{16,208},{32,224},{48,240},{64,0},{80,16},{96,32},{112,48}... | collective-permute-start | bytes 589832 | tf_op jit(solution)/shard_map/ppermute | solution.py:39
  65.5 8.8 %collective-permute-start.11 = (bf16[1,192,512]{2,1,0:T(8,128)(2,1)S(1)}, bf16[1,192,512]{2,1,0:T(8,128)(2,1)S(1)}, u32[]{:S(2)}, u32[]{:S(2)}) collective-permute-start(bf16[1,192,512]{2,1,0:T(8,128)(2,1)S(1)} %slice.6), channel_id=1, source_target_pairs={{0,64},{16,80},{32,96},{48,112},{64,128},{80,144},{96,160},{112,17... | collective-permute-start | bytes 589832 | tf_op jit(solution)/shard_map/ppermute | solution.py:39
  65.6 10.2 %collective-permute-start.10 = (bf16[2,192,512]{2,1,0:T(8,128)(2,1)S(1)}, bf16[2,192,512]{2,1,0:T(8,128)(2,1)S(1)}, u32[]{:S(2)}, u32[]{:S(2)}) collective-permute-start(bf16[2,192,512]{2,1,0:T(8,128)(2,1)S(1)} %collective-permute-done.7.refs_1_), channel_id=1, source_target_pairs={{0,16},{16,0},{32,48},{48,32},{64,80},{80,64},{96,112},{112,96},{1... | collective-permute-start | bytes 1179656 | tf_op jit(solution)/shard_map/ppermute | solution.py:39
  65.7 10.1 %collective-permute-start.16 = (bf16[2,192,512]{2,1,0:T(8,128)(2,1)S(1)}, bf16[2,192,512]{2,1,0:T(8,128)(2,1)S(1)}, u32[]{:S(2)}, u32[]{:S(2)}) collective-permute-start(bf16[2,192,512]{2,1,0:T(8,128)(2,1)S(1)} %collective-permute-done.8.refs_4_), channel_id=1, source_target_pairs={{0,16},{16,0},{32,48},{48,32},{64,80},{80,64},{96,112},{112,96},{1... | collective-permute-start | bytes 1179656 | tf_op jit(solution)/shard_map/ppermute | solution.py:39
  66.2 9.6 %collective-permute-start.9 = (bf16[2,192,512]{2,1,0:T(8,128)(2,1)S(1)}, bf16[2,192,512]{2,1,0:T(8,128)(2,1)S(1)}, u32[]{:S(2)}, u32[]{:S(2)}) collective-permute-start(bf16[2,192,512]{2,1,0:T(8,128)(2,1)S(1)} %pad_maximum_fusion.1.refs_0_), channel_id=1, source_target_pairs={{0,16},{16,0},{32,48},{48,32},{64,80},{80,64},{96,112},{112,96},{1... | collective-permute-start | bytes 1179656 | tf_op jit(solution)/shard_map/ppermute | solution.py:39
  82.5 7.8 %collective-permute-start.17 = (bf16[128,256]{1,0:T(8,128)(2,1)S(1)}, bf16[128,256]{1,0:T(8,128)(2,1)S(1)}, u32[]{:S(2)}, u32[]{:S(2)}) collective-permute-start(bf16[128,256]{1,0:T(8,128)(2,1)S(1)} %attend.2.refs_0_), channel_id=1, source_target_pairs={{0,4},{1,5},{2,6},{3,7},{4,8},{5,9},{6,10},{7,11},{8,12},{9,13},{1... | collective-permute-start | bytes 196616 | tf_op jit(solution)/shard_map/ppermute | solution.py:28
  85.8 11.1 %collective-permute-start.18 = (bf16[128,256]{1,0:T(8,128)(2,1)S(1)}, bf16[128,256]{1,0:T(8,128)(2,1)S(1)}, u32[]{:S(2)}, u32[]{:S(2)}) collective-permute-start(bf16[128,256]{1,0:T(8,128)(2,1)S(1)} %attend.2.refs_0_), channel_id=1, source_target_pairs={{0,8},{1,9},{2,10},{3,11},{4,12},{5,13},{6,14},{7,15},{8,0},{9,1},... | collective-permute-start | bytes 196616 | tf_op jit(solution)/shard_map/ppermute | solution.py:28
  87.6 9.3 %collective-permute-start.19 = (bf16[128,256]{1,0:T(8,128)(2,1)S(1)}, bf16[128,256]{1,0:T(8,128)(2,1)S(1)}, u32[]{:S(2)}, u32[]{:S(2)}) collective-permute-start(bf16[128,256]{1,0:T(8,128)(2,1)S(1)} %attend.2.refs_0_), channel_id=1, source_target_pairs={{0,12},{1,13},{2,14},{3,15},{4,0},{5,1},{6,2},{7,3},{8,4},{9,5},{1... | collective-permute-start | bytes 196616 | tf_op jit(solution)/shard_map/ppermute | solution.py:28
  97.7 7.0 %collective-permute-start.20 = (bf16[192,256]{1,0:T(8,128)(2,1)S(1)}, bf16[192,256]{1,0:T(8,128)(2,1)S(1)}, u32[]{:S(2)}, u32[]{:S(2)}) collective-permute-start(bf16[192,256]{1,0:T(8,128)(2,1)S(1)} %get-tuple-element.82), channel_id=1, source_target_pairs={{0,1},{1,2},{2,3},{3,0},{4,5},{5,6},{6,7},{7,4},{8,9},{9,10},{10,1... | collective-permute-start | bytes 294920 | tf_op jit(solution)/shard_map/ppermute | solution.py:28
  97.9 7.7 %collective-permute-start.22 = (bf16[192,256]{1,0:T(8,128)(2,1)S(1)}, bf16[192,256]{1,0:T(8,128)(2,1)S(1)}, u32[]{:S(2)}, u32[]{:S(2)}) collective-permute-start(bf16[192,256]{1,0:T(8,128)(2,1)S(1)} %get-tuple-element.84), channel_id=1, source_target_pairs={{0,3},{1,0},{2,1},{3,2},{4,7},{5,4},{6,5},{7,6},{8,11},{9,8},{10,9... | collective-permute-start | bytes 294920 | tf_op jit(solution)/shard_map/ppermute | solution.py:28
  107.1 9.5 %collective-permute-start.24 = (bf16[192,256]{1,0:T(8,128)(2,1)S(1)}, bf16[192,256]{1,0:T(8,128)(2,1)S(1)}, u32[]{:S(2)}, u32[]{:S(2)}) collective-permute-start(bf16[192,256]{1,0:T(8,128)(2,1)S(1)} %update.2.x), channel_id=1, source_target_pairs={{0,8},{1,9},{2,10},{3,11},{4,12},{5,13},{6,14},{7,15},{8,0},{9,1},... | collective-permute-start | bytes 294920 | tf_op jit(solution)/shard_map/ppermute | solution.py:28
  108.3 8.3 %collective-permute-start.25 = (bf16[192,256]{1,0:T(8,128)(2,1)S(1)}, bf16[192,256]{1,0:T(8,128)(2,1)S(1)}, u32[]{:S(2)}, u32[]{:S(2)}) collective-permute-start(bf16[192,256]{1,0:T(8,128)(2,1)S(1)} %update.2.x), channel_id=1, source_target_pairs={{0,12},{1,13},{2,14},{3,15},{4,0},{5,1},{6,2},{7,3},{8,4},{9,5},{1... | collective-permute-start | bytes 294920 | tf_op jit(solution)/shard_map/ppermute | solution.py:28
  116.6 12.2 %collective-permute-start.26 = (bf16[4,192,256]{2,1,0:T(8,128)(2,1)S(1)}, bf16[4,192,256]{2,1,0:T(8,128)(2,1)S(1)}, u32[]{:S(2)}, u32[]{:S(2)}) collective-permute-start(bf16[4,192,256]{2,1,0:T(8,128)(2,1)S(1)} %pad_maximum_fusion.2.refs_0_), channel_id=1, source_target_pairs={{0,1},{1,2},{2,3},{3,0},{4,5},{5,6},{6,7},{7,4},{8,9},{9,10},{10,1... | collective-permute-start | bytes 1179656 | tf_op jit(solution)/shard_map/ppermute | solution.py:28
  117.4 18.6 %collective-permute-start.27 = (bf16[4,192,256]{2,1,0:T(8,128)(2,1)S(1)}, bf16[4,192,256]{2,1,0:T(8,128)(2,1)S(1)}, u32[]{:S(2)}, u32[]{:S(2)}) collective-permute-start(bf16[4,192,256]{2,1,0:T(8,128)(2,1)S(1)} %pad_maximum_fusion.2.refs_0_), channel_id=1, source_target_pairs={{0,2},{1,3},{2,0},{3,1},{4,6},{5,7},{6,4},{7,5},{8,10},{9,11},{10,... | collective-permute-start | bytes 1179656 | tf_op jit(solution)/shard_map/ppermute | solution.py:28
  121.2 14.8 %collective-permute-start.28 = (bf16[4,192,256]{2,1,0:T(8,128)(2,1)S(1)}, bf16[4,192,256]{2,1,0:T(8,128)(2,1)S(1)}, u32[]{:S(2)}, u32[]{:S(2)}) collective-permute-start(bf16[4,192,256]{2,1,0:T(8,128)(2,1)S(1)} %pad_maximum_fusion.2.refs_0_), channel_id=1, source_target_pairs={{0,3},{1,0},{2,1},{3,2},{4,7},{5,4},{6,5},{7,6},{8,11},{9,8},{10,9... | collective-permute-start | bytes 1179656 | tf_op jit(solution)/shard_map/ppermute | solution.py:28
  146.5 17.5 %collective-permute-start.29 = (bf16[128,256]{1,0:T(8,128)(2,1)S(1)}, bf16[128,256]{1,0:T(8,128)(2,1)S(1)}, u32[]{:S(2)}, u32[]{:S(2)}) collective-permute-start(bf16[128,256]{1,0:T(8,128)(2,1)S(1)} %attend.3.refs_0_), channel_id=1, source_target_pairs={{0,4},{1,5},{2,6},{3,7},{4,8},{5,9},{6,10},{7,11},{8,12},{9,13},{1... | collective-permute-start | bytes 196616 | tf_op jit(solution)/shard_map/ppermute | solution.py:28
  149.7 16.3 %collective-permute-start.30 = (bf16[128,256]{1,0:T(8,128)(2,1)S(1)}, bf16[128,256]{1,0:T(8,128)(2,1)S(1)}, u32[]{:S(2)}, u32[]{:S(2)}) collective-permute-start(bf16[128,256]{1,0:T(8,128)(2,1)S(1)} %attend.3.refs_0_), channel_id=1, source_target_pairs={{0,8},{1,9},{2,10},{3,11},{4,12},{5,13},{6,14},{7,15},{8,0},{9,1},... | collective-permute-start | bytes 196616 | tf_op jit(solution)/shard_map/ppermute | solution.py:28
  169.1 7.0 %collective-permute-start.32 = (bf16[192,256]{1,0:T(8,128)(2,1)S(1)}, bf16[192,256]{1,0:T(8,128)(2,1)S(1)}, u32[]{:S(2)}, u32[]{:S(2)}) collective-permute-start(bf16[192,256]{1,0:T(8,128)(2,1)S(1)} %get-tuple-element.92), channel_id=1, source_target_pairs={{0,1},{1,2},{2,3},{3,0},{4,5},{5,6},{6,7},{7,4},{8,9},{9,10},{10,1... | collective-permute-start | bytes 294920 | tf_op jit(solution)/shard_map/ppermute | solution.py:28
  169.3 7.9 %collective-permute-start.33 = (bf16[192,256]{1,0:T(8,128)(2,1)S(1)}, bf16[192,256]{1,0:T(8,128)(2,1)S(1)}, u32[]{:S(2)}, u32[]{:S(2)}) collective-permute-start(bf16[192,256]{1,0:T(8,128)(2,1)S(1)} %get-tuple-element.93), channel_id=1, source_target_pairs={{0,2},{1,3},{2,0},{3,1},{4,6},{5,7},{6,4},{7,5},{8,10},{9,11},{10,... | collective-permute-start | bytes 294920 | tf_op jit(solution)/shard_map/ppermute | solution.py:28
  (19 other events, 147.7 us)
Sparse Core Ops, SparseCore 0:
  10.7 64.6 all-gather.3
  78.6 57.4 all-gather.5

commit v3 on v1

--- a/solution.py
+++ b/solution.py
@@ -297,7 +297,11 @@
             break
         x_l = shifts(x, "l", NL)
         x_four = jnp.stack([x] + x_l)
-        groups = [x_four] + shifts(x_four, "x", NX)
+        x_up, x_down = shift(x_four, "x", 1), shift(x_four, "x", 3)
+        x_up, x_down, x_four = sync(x_up, x_down, x_four)
+        half = NL // 2
+        x_far = jnp.concatenate([shift(x_up[:half], "x", 1), shift(x_down[half:], "x", 3)])
+        groups = [x_four, x_up, x_far, x_down]
         normed = norm(step + 1, groups)
         past = kv_all
     return x.T, kv.reshape(2, tok, size)

time: 178 us -> 178 us (level)
    ppermute x24 -> x25, waiting for transfers between devices: 42.6 us -> 40 us  [shift(): return lax.ppermute(array, 'tp', pairs)]
    ppermute x24 -> x25, starting transfers between devices: 33.5 us -> 34.9 us  [shift(): return lax.ppermute(array, 'tp', pairs)]
  transfers between devices with their start and end apart: 38 -> 39, of which waited for: 20 -> 21; matrix products, arithmetic and copies ran while one was open for 2% -> 2% of each run, Pallas kernels for 8% -> 8%
where the time goes in v3:
time: 178 us; the launch traced here: 177 us
  waiting for transfers between devices  74.3 us (42%)
  starting transfers between devices  60 us (34%)
  Pallas kernels  19.6 us (11%)
  between operations  14.3 us (8%)
  local copies, waits for them, and re-layouts  7.92 us (4%)
    ppermute x25, waiting for transfers between devices, shift(): return lax.ppermute(array, 'tp', pairs)  40 us
    ppermute x25, starting transfers between devices, shift(): return lax.ppermute(array, 'tp', pairs)  34.9 us
    pallas_call x11, Pallas kernels, call(): pl.pallas_call(body, out_shape=outs, in_specs=[pl.BlockSpec(memory_space=...  19.6 us
    ppermute x10, waiting for transfers between devices, shift(): return lax.ppermute(array, 'patch', pairs)  17.8 us
    ppermute x10, starting transfers between devices, shift(): return lax.ppermute(array, 'patch', pairs)  11.8 us
    all_to_all x1, starting transfers between devices, on_device(): w_mine = lax.all_to_all(sent, 'tp', 0, 0)  8.85 us
    ppermute x1, waiting for transfers between devices, swap(): return lax.ppermute(array, ('patch', 'tp'), pairs)  6.65 us
    unnamed x28, local copies, waits for them, and re-layouts  5.77 us
  transfers between devices with their start and end apart: 39, of which 21 were waited for; matrix products, arithmetic and copies ran while one was open for 2% of the time, Pallas kernels for 8%

profile of v3, /device:TPU:6, one launch (start us, length us, event | category | flops | bytes accessed | tf_op | source)
XLA Modules:
  0.0 177.3 jit_solution(9512718045217020723)
XLA Ops:
  9.7 8.9 %all-to-all-start = ((bf16[16,36,128]{2,1,0:T(8,128)(2,1)}), bf16[16,36,128]{2,1,0:T(8,128)(2,1)S(1)}, u32[]{:S(2)}, u32[]{:S(2)}) async-start(bf16[16,36,128]{2,1,0:T(8,128)(2,1)} %copy.14), calls=%async_computation | async-start | bytes 327680 | tf_op jit(solution)/shard_map/all_to_all | solution.py:220
  20.2 2.4 %collective-permute-start.1 = (bf16[192,256]{1,0:T(8,128)(2,1)}, bf16[192,256]{1,0:T(8,128)(2,1)S(1)}, u32[]{:S(2)}, u32[]{:S(2)}) collective-permute-start(bf16[192,256]{1,0:T(8,128)(2,1)} %bitcast.32), channel_id=1, source_target_pairs={{0,8},{1,9},{2,10},{3,11},{4,12},{5,13},{6,14},{7,15},{8,0},{9,1},... | collective-permute-start | bytes 294920 | tf_op jit(solution)/shard_map/ppermute | solution.py:28
  24.0 4.4 %collective-permute-start.3 = (bf16[192,128]{1,0:T(8,128)(2,1)}, bf16[192,128]{1,0:T(8,128)(2,1)S(1)}, u32[]{:S(2)}, u32[]{:S(2)}) collective-permute-start(bf16[192,128]{1,0:T(8,128)(2,1)} %param.11), channel_id=1, source_target_pairs={{0,0},{1,16},{2,32},{3,48},{4,4},{5,20},{6,36},{7,52},{8,8},{9,24}... | collective-permute-start | bytes 147464 | tf_op jit(solution)/shard_map/ppermute | solution.py:192
  29.5 6.7 %collective-permute-done.3 = bf16[192,128]{1,0:T(8,128)(2,1)S(1)} collective-permute-done((bf16[192,128]{1,0:T(8,128)(2,1)}, bf16[192,128]{1,0:T(8,128)(2,1)S(1)}, u32[]{:S(2)}, u32[]{:S(2)}) %collective-permute-start.3) | collective-permute-done | bytes 49184 | tf_op jit(solution)/shard_map/ppermute | solution.py:192
  39.5 4.0 %collective-permute-start.4 = (bf16[192,512]{1,0:T(8,128)(2,1)S(1)}, bf16[192,512]{1,0:T(8,128)(2,1)S(1)}, u32[]{:S(2)}, u32[]{:S(2)}) collective-permute-start(bf16[192,512]{1,0:T(8,128)(2,1)S(1)} %constant_dynamic-update-slice_fusion), channel_id=1, source_target_pairs={{0,32},{16,48},{32,0},{48,16},{64,96},{80,112},{96,64},{112,80},{1... | collective-permute-start | bytes 589832 | tf_op jit(solution)/shard_map/ppermute | solution.py:39
  43.4 5.8 %collective-permute-done.4 = bf16[192,512]{1,0:T(8,128)(2,1)S(1)} collective-permute-done((bf16[192,512]{1,0:T(8,128)(2,1)S(1)}, bf16[192,512]{1,0:T(8,128)(2,1)S(1)}, u32[]{:S(2)}, u32[]{:S(2)}) %collective-permute-start.4) | collective-permute-done | bytes 196640 | tf_op jit(solution)/shard_map/ppermute | solution.py:39
  54.0 6.6 %collective-permute-done.7.refs_1_ = bf16[2,192,512]{2,1,0:T(8,128)(2,1)S(1)} collective-permute-done((bf16[2,192,512]{2,1,0:T(8,128)(2,1)S(1)}, bf16[2,192,512]{2,1,0:T(8,128)(2,1)S(1)}, u32[]{:S(2)}, u32[]{:S(2)}) %collective-permute-start.7) | collective-permute-done | bytes 393248 | tf_op jit(solution)/shard_map/ppermute | solution.py:39
  64.7 5.4 %collective-permute-done.11.refs_2_ = bf16[1,192,512]{2,1,0:T(8,128)(2,1)S(1)} collective-permute-done((bf16[1,192,512]{2,1,0:T(8,128)(2,1)S(1)}, bf16[1,192,512]{2,1,0:T(8,128)(2,1)S(1)}, u32[]{:S(2)}, u32[]{:S(2)}) %collective-permute-start.11) | collective-permute-done | bytes 196640 | tf_op jit(solution)/shard_map/ppermute | solution.py:39
  70.6 2.2 %norm.2.normed = bf16[16,192,256]{2,1,0:T(8,128)(2,1)S(1)} custom-call(s32[2]{0:T(128)S(1)} %pad_add_fusion.ids, f32[96,192]{1,0:T(8,128)S(1)} %reshape.30.mod, bf16[4,192,256]{2,1,0:T(8,128)(2,1)S(1)} %pad_maximum_fusion.refs_0_, bf16[4,192,256]{2,1,0:T(8,128)(2,1)S(1)} %collective-permute-done.5.refs_1_, ...), custom_call_target="tpu_custom_call" | custom-call | flops 1048576 | bytes 4194304 | tf_op jit(solution)/shard_map/norm/pallas_call | solution.py:53
  72.9 2.7 %qkv.2 = (bf16[512,128]{1,0:T(8,128)(2,1)}, bf16[768,128]{1,0:T(8,128)(2,1)S(1)}) custom-call(s32[2]{0:T(128)S(1)} %pad_add_fusion.ids, bf16[16,192,256]{2,1,0:T(8,128)(2,1)S(1)} %norm.2.normed, f32[1,128]{1,0:T(1,128)S(1)} %bitcast.36, f32[1,128]{1,0:T(1,128)S(1)} %bitcast.38, bf16[2,192,512]{2,1,0:T(8,128)(2,1)S(1)} %pad_maximum_fusion.1.refs_0_, ...), custom_call_target="tpu_custom_call" | custom-call | flops 1048576 | bytes 16777216 | tf_op jit(solution)/shard_map/qkv/pallas_call | solution.py:53
  75.6 5.0 %all-gather.4.cloned.1.call-done.past = bf16[16,512,128]{2,1,0:T(8,128)(2,1)} async-done(((bf16[1,512,128]{2,1,0:T(8,128)(2,1)}), bf16[16,512,128]{2,1,0:T(8,128)(2,1)}) %all-gather.4.cloned.1.call-update) | async-done | bytes 2097168 | tf_op jit(solution)/shard_map/all_gather | solution.py:222
  82.2 2.4 %attend.2.refs_0_ = bf16[128,256]{1,0:T(8,128)(2,1)S(1)} custom-call(s32[2]{0:T(128)S(1)} %pad_add_fusion.ids, bf16[768,128]{1,0:T(8,128)(2,1)S(1)} %get-tuple-element.75.near, bf16[16,512,128]{2,1,0:T(8,128)(2,1)S(1)} %copy-done), custom_call_target="tpu_custom_call" | custom-call | flops 1048576 | bytes 8388608 | tf_op jit(solution)/shard_map/attend/pallas_call | solution.py:53
  84.6 2.4 %collective-permute-start.17 = (bf16[128,256]{1,0:T(8,128)(2,1)S(1)}, bf16[128,256]{1,0:T(8,128)(2,1)S(1)}, u32[]{:S(2)}, u32[]{:S(2)}) collective-permute-start(bf16[128,256]{1,0:T(8,128)(2,1)S(1)} %attend.2.refs_0_), channel_id=1, source_target_pairs={{0,4},{1,5},{2,6},{3,7},{4,8},{5,9},{6,10},{7,11},{8,12},{9,13},{1... | collective-permute-start | bytes 196616 | tf_op jit(solution)/shard_map/ppermute | solution.py:28
  88.6 2.8 %collective-permute-start.19 = (bf16[128,256]{1,0:T(8,128)(2,1)S(1)}, bf16[128,256]{1,0:T(8,128)(2,1)S(1)}, u32[]{:S(2)}, u32[]{:S(2)}) collective-permute-start(bf16[128,256]{1,0:T(8,128)(2,1)S(1)} %attend.2.refs_0_), channel_id=1, source_target_pairs={{0,12},{1,13},{2,14},{3,15},{4,0},{5,1},{6,2},{7,3},{8,4},{9,5},{1... | collective-permute-start | bytes 196616 | tf_op jit(solution)/shard_map/ppermute | solution.py:28
  95.1 2.2 %collective-permute-start.20 = (bf16[192,256]{1,0:T(8,128)(2,1)S(1)}, bf16[192,256]{1,0:T(8,128)(2,1)S(1)}, u32[]{:S(2)}, u32[]{:S(2)}) collective-permute-start(bf16[192,256]{1,0:T(8,128)(2,1)S(1)} %get-tuple-element.81), channel_id=1, source_target_pairs={{0,1},{1,2},{2,3},{3,0},{4,5},{5,6},{6,7},{7,4},{8,9},{9,10},{10,1... | collective-permute-start | bytes 294920 | tf_op jit(solution)/shard_map/ppermute | solution.py:28
  98.4 2.2 %collective-permute-done.20.refs_0_ = bf16[192,256]{1,0:T(8,128)(2,1)S(1)} collective-permute-done((bf16[192,256]{1,0:T(8,128)(2,1)S(1)}, bf16[192,256]{1,0:T(8,128)(2,1)S(1)}, u32[]{:S(2)}, u32[]{:S(2)}) %collective-permute-start.20) | collective-permute-done | bytes 98336 | tf_op jit(solution)/shard_map/ppermute | solution.py:28
  100.7 2.9 %collective-permute-done.21.refs_1_ = bf16[192,256]{1,0:T(8,128)(2,1)S(1)} collective-permute-done((bf16[192,256]{1,0:T(8,128)(2,1)S(1)}, bf16[192,256]{1,0:T(8,128)(2,1)S(1)}, u32[]{:S(2)}, u32[]{:S(2)}) %collective-permute-start.21) | collective-permute-done | bytes 98336 | tf_op jit(solution)/shard_map/ppermute | solution.py:28
  105.5 2.0 %collective-permute-start.23 = (bf16[192,256]{1,0:T(8,128)(2,1)S(1)}, bf16[192,256]{1,0:T(8,128)(2,1)S(1)}, u32[]{:S(2)}, u32[]{:S(2)}) collective-permute-start(bf16[192,256]{1,0:T(8,128)(2,1)S(1)} %update.2.x), channel_id=1, source_target_pairs={{0,4},{1,5},{2,6},{3,7},{4,8},{5,9},{6,10},{7,11},{8,12},{9,13},{1... | collective-permute-start | bytes 294920 | tf_op jit(solution)/shard_map/ppermute | solution.py:28
  107.5 2.0 %collective-permute-start.24 = (bf16[192,256]{1,0:T(8,128)(2,1)S(1)}, bf16[192,256]{1,0:T(8,128)(2,1)S(1)}, u32[]{:S(2)}, u32[]{:S(2)}) collective-permute-start(bf16[192,256]{1,0:T(8,128)(2,1)S(1)} %update.2.x), channel_id=1, source_target_pairs={{0,8},{1,9},{2,10},{3,11},{4,12},{5,13},{6,14},{7,15},{8,0},{9,1},... | collective-permute-start | bytes 294920 | tf_op jit(solution)/shard_map/ppermute | solution.py:28
  110.0 3.1 %collective-permute-done.23 = bf16[192,256]{1,0:T(8,128)(2,1)S(1)} collective-permute-done((bf16[192,256]{1,0:T(8,128)(2,1)S(1)}, bf16[192,256]{1,0:T(8,128)(2,1)S(1)}, u32[]{:S(2)}, u32[]{:S(2)}) %collective-permute-start.23) | collective-permute-done | bytes 98336 | tf_op jit(solution)/shard_map/ppermute | solution.py:28
  113.1 2.6 %collective-permute-done.24 = bf16[192,256]{1,0:T(8,128)(2,1)S(1)} collective-permute-done((bf16[192,256]{1,0:T(8,128)(2,1)S(1)}, bf16[192,256]{1,0:T(8,128)(2,1)S(1)}, u32[]{:S(2)}, u32[]{:S(2)}) %collective-permute-start.24) | collective-permute-done | bytes 98336 | tf_op jit(solution)/shard_map/ppermute | solution.py:28
  118.1 8.8 %collective-permute-done.26.refs_1_ = bf16[4,192,256]{2,1,0:T(8,128)(2,1)S(1)} collective-permute-done((bf16[4,192,256]{2,1,0:T(8,128)(2,1)S(1)}, bf16[4,192,256]{2,1,0:T(8,128)(2,1)S(1)}, u32[]{:S(2)}, u32[]{:S(2)}) %collective-permute-start.26) | collective-permute-done | bytes 393248 | tf_op jit(solution)/shard_map/ppermute | solution.py:28
  130.5 3.7 %collective-permute-done.28 = bf16[2,192,256]{2,1,0:T(8,128)(2,1)S(1)} collective-permute-done((bf16[2,192,256]{2,1,0:T(8,128)(2,1)S(1)}, bf16[2,192,256]{2,1,0:T(8,128)(2,1)S(1)}, u32[]{:S(2)}, u32[]{:S(2)}) %collective-permute-start.28) | collective-permute-done | bytes 196640 | tf_op jit(solution)/shard_map/ppermute | solution.py:28
  135.6 2.2 %norm.3.normed = bf16[16,192,256]{2,1,0:T(8,128)(2,1)S(1)} custom-call(s32[2]{0:T(128)S(1)} %pad_add_fusion.ids, f32[96,192]{1,0:T(8,128)S(1)} %reshape.30.mod, bf16[4,192,256]{2,1,0:T(8,128)(2,1)S(1)} %pad_maximum_fusion.2.refs_0_, bf16[4,192,256]{2,1,0:T(8,128)(2,1)S(1)} %collective-permute-done.26.refs_1_, ...), custom_call_target="tpu_custom_call" | custom-call | flops 1048576 | bytes 4194304 | tf_op jit(solution)/shard_map/norm/pallas_call | solution.py:53
  137.9 2.7 %qkv.3 = (bf16[512,128]{1,0:T(8,128)(2,1)}, bf16[768,128]{1,0:T(8,128)(2,1)S(1)}) custom-call(s32[2]{0:T(128)S(1)} %pad_add_fusion.ids, bf16[16,192,256]{2,1,0:T(8,128)(2,1)S(1)} %norm.3.normed, f32[1,128]{1,0:T(1,128)S(1)} %bitcast.37, f32[1,128]{1,0:T(1,128)S(1)} %bitcast.39, bf16[2,192,512]{2,1,0:T(8,128)(2,1)S(1)} %pad_maximum_fusion.1.refs_0_, ...), custom_call_target="tpu_custom_call" | custom-call | flops 1048576 | bytes 16777216 | tf_op jit(solution)/shard_map/qkv/pallas_call | solution.py:53
  141.2 4.1 %all-gather.6.cloned.1.call-done = bf16[8192,128]{1,0:T(8,128)(2,1)} async-done(((bf16[512,128]{1,0:T(8,128)(2,1)}), bf16[8192,128]{1,0:T(8,128)(2,1)}) %all-gather.6.cloned.1.call-update) | async-done | bytes 2097168 | tf_op jit(solution)/shard_map/all_gather | solution.py:255
  147.9 2.4 %attend.3.refs_0_ = bf16[128,256]{1,0:T(8,128)(2,1)S(1)} custom-call(s32[2]{0:T(128)S(1)} %pad_add_fusion.ids, bf16[768,128]{1,0:T(8,128)(2,1)S(1)} %copy-done.10, bf16[16,512,128]{2,1,0:T(8,128)(2,1)S(1)} %bitcast.29), custom_call_target="tpu_custom_call" | custom-call | flops 1048576 | bytes 8388608 | tf_op jit(solution)/shard_map/attend/pallas_call | solution.py:53
  151.0 3.2 %collective-permute-start.32 = (bf16[128,256]{1,0:T(8,128)(2,1)S(1)}, bf16[128,256]{1,0:T(8,128)(2,1)S(1)}, u32[]{:S(2)}, u32[]{:S(2)}) collective-permute-start(bf16[128,256]{1,0:T(8,128)(2,1)S(1)} %attend.3.refs_0_), channel_id=1, source_target_pairs={{0,12},{1,13},{2,14},{3,15},{4,0},{5,1},{6,2},{7,3},{8,4},{9,5},{1... | collective-permute-start | bytes 196616 | tf_op jit(solution)/shard_map/ppermute | solution.py:28
  154.2 3.0 %collective-permute-done.30.refs_1_ = bf16[128,256]{1,0:T(8,128)(2,1)S(1)} collective-permute-done((bf16[128,256]{1,0:T(8,128)(2,1)S(1)}, bf16[128,256]{1,0:T(8,128)(2,1)S(1)}, u32[]{:S(2)}, u32[]{:S(2)}) %collective-permute-start.30) | collective-permute-done | bytes 65568 | tf_op jit(solution)/shard_map/ppermute | solution.py:28
  157.2 2.1 %collective-permute-done.31.refs_2_ = bf16[128,256]{1,0:T(8,128)(2,1)S(1)} collective-permute-done((bf16[128,256]{1,0:T(8,128)(2,1)S(1)}, bf16[128,256]{1,0:T(8,128)(2,1)S(1)}, u32[]{:S(2)}, u32[]{:S(2)}) %collective-permute-start.31) | collective-permute-done | bytes 65568 | tf_op jit(solution)/shard_map/ppermute | solution.py:28
  160.9 2.4 %collective-permute-start.34 = (bf16[192,256]{1,0:T(8,128)(2,1)S(1)}, bf16[192,256]{1,0:T(8,128)(2,1)S(1)}, u32[]{:S(2)}, u32[]{:S(2)}) collective-permute-start(bf16[192,256]{1,0:T(8,128)(2,1)S(1)} %get-tuple-element.95), channel_id=1, source_target_pairs={{0,2},{1,3},{2,0},{3,1},{4,6},{5,7},{6,4},{7,5},{8,10},{9,11},{10,... | collective-permute-start | bytes 294920 | tf_op jit(solution)/shard_map/ppermute | solution.py:28
  164.9 2.4 %collective-permute-done.34.refs_1_ = bf16[192,256]{1,0:T(8,128)(2,1)S(1)} collective-permute-done((bf16[192,256]{1,0:T(8,128)(2,1)S(1)}, bf16[192,256]{1,0:T(8,128)(2,1)S(1)}, u32[]{:S(2)}, u32[]{:S(2)}) %collective-permute-start.34) | collective-permute-done | bytes 98336 | tf_op jit(solution)/shard_map/ppermute | solution.py:28
  (103 shorter events, 47.3 us)
Async XLA Ops:
  7.2 73.4 %all-gather.4.cloned.1.call-start = ((), (), s32[]{:S(2)}) async-start(), calls=%async_computation.1 | async-start | bytes 2228224 | tf_op jit(solution)/shard_map/all_gather | solution.py:222
  9.7 26.5 %all-to-all-start = ((bf16[16,36,128]{2,1,0:T(8,128)(2,1)}), bf16[16,36,128]{2,1,0:T(8,128)(2,1)S(1)}, u32[]{:S(2)}, u32[]{:S(2)}) async-start(bf16[16,36,128]{2,1,0:T(8,128)(2,1)} %copy.14), calls=%async_computation | async-start | bytes 327680 | tf_op jit(solution)/shard_map/all_to_all | solution.py:220
  18.6 126.8 %all-gather.6.cloned.1.call-start = ((), (), s32[]{:S(2)}) async-start(), calls=%async_computation.2 | async-start | bytes 2228224 | tf_op jit(solution)/shard_map/all_gather | solution.py:255
  18.6 17.6 %collective-permute-start = (bf16[192,256]{1,0:T(8,128)(2,1)}, bf16[192,256]{1,0:T(8,128)(2,1)S(1)}, u32[]{:S(2)}, u32[]{:S(2)}) collective-permute-start(bf16[192,256]{1,0:T(8,128)(2,1)} %bitcast.31), channel_id=1, source_target_pairs={{0,4},{1,5},{2,6},{3,7},{4,8},{5,9},{6,10},{7,11},{8,12},{9,13},{1... | collective-permute-start | bytes 294920 | tf_op jit(solution)/shard_map/ppermute | solution.py:28
  20.2 16.0 %collective-permute-start.1 = (bf16[192,256]{1,0:T(8,128)(2,1)}, bf16[192,256]{1,0:T(8,128)(2,1)S(1)}, u32[]{:S(2)}, u32[]{:S(2)}) collective-permute-start(bf16[192,256]{1,0:T(8,128)(2,1)} %bitcast.32), channel_id=1, source_target_pairs={{0,8},{1,9},{2,10},{3,11},{4,12},{5,13},{6,14},{7,15},{8,0},{9,1},... | collective-permute-start | bytes 294920 | tf_op jit(solution)/shard_map/ppermute | solution.py:28
  22.5 13.7 %collective-permute-start.2 = (bf16[192,256]{1,0:T(8,128)(2,1)}, bf16[192,256]{1,0:T(8,128)(2,1)S(1)}, u32[]{:S(2)}, u32[]{:S(2)}) collective-permute-start(bf16[192,256]{1,0:T(8,128)(2,1)} %bitcast.33), channel_id=1, source_target_pairs={{0,12},{1,13},{2,14},{3,15},{4,0},{5,1},{6,2},{7,3},{8,4},{9,5},{1... | collective-permute-start | bytes 294920 | tf_op jit(solution)/shard_map/ppermute | solution.py:28
  24.0 12.2 %collective-permute-start.3 = (bf16[192,128]{1,0:T(8,128)(2,1)}, bf16[192,128]{1,0:T(8,128)(2,1)S(1)}, u32[]{:S(2)}, u32[]{:S(2)}) collective-permute-start(bf16[192,128]{1,0:T(8,128)(2,1)} %param.11), channel_id=1, source_target_pairs={{0,0},{1,16},{2,32},{3,48},{4,4},{5,20},{6,36},{7,52},{8,8},{9,24}... | collective-permute-start | bytes 147464 | tf_op jit(solution)/shard_map/ppermute | solution.py:192
  37.2 12.1 %collective-permute-start.5 = (bf16[4,192,256]{2,1,0:T(8,128)(2,1)S(1)}, bf16[4,192,256]{2,1,0:T(8,128)(2,1)S(1)}, u32[]{:S(2)}, u32[]{:S(2)}) collective-permute-start(bf16[4,192,256]{2,1,0:T(8,128)(2,1)S(1)} %pad_maximum_fusion.refs_0_), channel_id=1, source_target_pairs={{0,1},{1,2},{2,3},{3,0},{4,5},{5,6},{6,7},{7,4},{8,9},{9,10},{10,1... | collective-permute-start | bytes 1179656 | tf_op jit(solution)/shard_map/ppermute | solution.py:28
  37.3 12.0 %collective-permute-start.6 = (bf16[4,192,256]{2,1,0:T(8,128)(2,1)S(1)}, bf16[4,192,256]{2,1,0:T(8,128)(2,1)S(1)}, u32[]{:S(2)}, u32[]{:S(2)}) collective-permute-start(bf16[4,192,256]{2,1,0:T(8,128)(2,1)S(1)} %pad_maximum_fusion.refs_0_), channel_id=1, source_target_pairs={{0,3},{1,0},{2,1},{3,2},{4,7},{5,4},{6,5},{7,6},{8,11},{9,8},{10,9... | collective-permute-start | bytes 1179656 | tf_op jit(solution)/shard_map/ppermute | solution.py:28
  39.5 9.8 %collective-permute-start.4 = (bf16[192,512]{1,0:T(8,128)(2,1)S(1)}, bf16[192,512]{1,0:T(8,128)(2,1)S(1)}, u32[]{:S(2)}, u32[]{:S(2)}) collective-permute-start(bf16[192,512]{1,0:T(8,128)(2,1)S(1)} %constant_dynamic-update-slice_fusion), channel_id=1, source_target_pairs={{0,32},{16,48},{32,0},{48,16},{64,96},{80,112},{96,64},{112,80},{1... | collective-permute-start | bytes 589832 | tf_op jit(solution)/shard_map/ppermute | solution.py:39
  49.3 11.3 %collective-permute-start.7 = (bf16[2,192,512]{2,1,0:T(8,128)(2,1)S(1)}, bf16[2,192,512]{2,1,0:T(8,128)(2,1)S(1)}, u32[]{:S(2)}, u32[]{:S(2)}) collective-permute-start(bf16[2,192,512]{2,1,0:T(8,128)(2,1)S(1)} %pad_maximum_fusion.1.refs_0_), channel_id=1, source_target_pairs={{0,64},{16,80},{32,96},{48,112},{64,128},{80,144},{96,160},{112,17... | collective-permute-start | bytes 1179656 | tf_op jit(solution)/shard_map/ppermute | solution.py:39
  51.0 9.6 %collective-permute-start.8 = (bf16[2,192,512]{2,1,0:T(8,128)(2,1)S(1)}, bf16[2,192,512]{2,1,0:T(8,128)(2,1)S(1)}, u32[]{:S(2)}, u32[]{:S(2)}) collective-permute-start(bf16[2,192,512]{2,1,0:T(8,128)(2,1)S(1)} %pad_maximum_fusion.1.refs_0_), channel_id=1, source_target_pairs={{0,192},{16,208},{32,224},{48,240},{64,0},{80,16},{96,32},{112,48}... | collective-permute-start | bytes 1179656 | tf_op jit(solution)/shard_map/ppermute | solution.py:39
  52.6 11.5 %collective-permute-start.16 = (bf16[4,192,256]{2,1,0:T(8,128)(2,1)S(1)}, bf16[4,192,256]{2,1,0:T(8,128)(2,1)S(1)}, u32[]{:S(2)}, u32[]{:S(2)}) collective-permute-start(bf16[4,192,256]{2,1,0:T(8,128)(2,1)S(1)} %pad_maximum_fusion.refs_0_), channel_id=1, source_target_pairs={{0,2},{1,3},{2,0},{3,1},{4,6},{5,7},{6,4},{7,5},{8,10},{9,11},{10,... | collective-permute-start | bytes 1179656 | tf_op jit(solution)/shard_map/ppermute | solution.py:28
  60.6 12.2 %collective-permute-start.10 = (bf16[2,192,512]{2,1,0:T(8,128)(2,1)S(1)}, bf16[2,192,512]{2,1,0:T(8,128)(2,1)S(1)}, u32[]{:S(2)}, u32[]{:S(2)}) collective-permute-start(bf16[2,192,512]{2,1,0:T(8,128)(2,1)S(1)} %collective-permute-done.7.refs_1_), channel_id=1, source_target_pairs={{0,16},{16,0},{32,48},{48,32},{64,80},{80,64},{96,112},{112,96},{1... | collective-permute-start | bytes 1179656 | tf_op jit(solution)/shard_map/ppermute | solution.py:39
  60.7 9.3 %collective-permute-start.11 = (bf16[1,192,512]{2,1,0:T(8,128)(2,1)S(1)}, bf16[1,192,512]{2,1,0:T(8,128)(2,1)S(1)}, u32[]{:S(2)}, u32[]{:S(2)}) collective-permute-start(bf16[1,192,512]{2,1,0:T(8,128)(2,1)S(1)} %slice.12), channel_id=1, source_target_pairs={{0,64},{16,80},{32,96},{48,112},{64,128},{80,144},{96,160},{112,17... | collective-permute-start | bytes 589832 | tf_op jit(solution)/shard_map/ppermute | solution.py:39
  62.2 7.8 %collective-permute-start.13 = (bf16[1,192,512]{2,1,0:T(8,128)(2,1)S(1)}, bf16[1,192,512]{2,1,0:T(8,128)(2,1)S(1)}, u32[]{:S(2)}, u32[]{:S(2)}) collective-permute-start(bf16[1,192,512]{2,1,0:T(8,128)(2,1)S(1)} %slice.13), channel_id=1, source_target_pairs={{0,192},{16,208},{32,224},{48,240},{64,0},{80,16},{96,32},{112,48}... | collective-permute-start | bytes 589832 | tf_op jit(solution)/shard_map/ppermute | solution.py:39
  64.1 8.7 %collective-permute-start.15 = (bf16[2,192,512]{2,1,0:T(8,128)(2,1)S(1)}, bf16[2,192,512]{2,1,0:T(8,128)(2,1)S(1)}, u32[]{:S(2)}, u32[]{:S(2)}) collective-permute-start(bf16[2,192,512]{2,1,0:T(8,128)(2,1)S(1)} %collective-permute-done.8.refs_4_), channel_id=1, source_target_pairs={{0,16},{16,0},{32,48},{48,32},{64,80},{80,64},{96,112},{112,96},{1... | collective-permute-start | bytes 1179656 | tf_op jit(solution)/shard_map/ppermute | solution.py:39
  64.2 8.7 %collective-permute-start.9 = (bf16[2,192,512]{2,1,0:T(8,128)(2,1)S(1)}, bf16[2,192,512]{2,1,0:T(8,128)(2,1)S(1)}, u32[]{:S(2)}, u32[]{:S(2)}) collective-permute-start(bf16[2,192,512]{2,1,0:T(8,128)(2,1)S(1)} %pad_maximum_fusion.1.refs_0_), channel_id=1, source_target_pairs={{0,16},{16,0},{32,48},{48,32},{64,80},{80,64},{96,112},{112,96},{1... | collective-permute-start | bytes 1179656 | tf_op jit(solution)/shard_map/ppermute | solution.py:39
  84.6 7.9 %collective-permute-start.17 = (bf16[128,256]{1,0:T(8,128)(2,1)S(1)}, bf16[128,256]{1,0:T(8,128)(2,1)S(1)}, u32[]{:S(2)}, u32[]{:S(2)}) collective-permute-start(bf16[128,256]{1,0:T(8,128)(2,1)S(1)} %attend.2.refs_0_), channel_id=1, source_target_pairs={{0,4},{1,5},{2,6},{3,7},{4,8},{5,9},{6,10},{7,11},{8,12},{9,13},{1... | collective-permute-start | bytes 196616 | tf_op jit(solution)/shard_map/ppermute | solution.py:28
  87.0 7.3 %collective-permute-start.18 = (bf16[128,256]{1,0:T(8,128)(2,1)S(1)}, bf16[128,256]{1,0:T(8,128)(2,1)S(1)}, u32[]{:S(2)}, u32[]{:S(2)}) collective-permute-start(bf16[128,256]{1,0:T(8,128)(2,1)S(1)} %attend.2.refs_0_), channel_id=1, source_target_pairs={{0,8},{1,9},{2,10},{3,11},{4,12},{5,13},{6,14},{7,15},{8,0},{9,1},... | collective-permute-start | bytes 196616 | tf_op jit(solution)/shard_map/ppermute | solution.py:28
  97.3 6.2 %collective-permute-start.21 = (bf16[192,256]{1,0:T(8,128)(2,1)S(1)}, bf16[192,256]{1,0:T(8,128)(2,1)S(1)}, u32[]{:S(2)}, u32[]{:S(2)}) collective-permute-start(bf16[192,256]{1,0:T(8,128)(2,1)S(1)} %get-tuple-element.82), channel_id=1, source_target_pairs={{0,2},{1,3},{2,0},{3,1},{4,6},{5,7},{6,4},{7,5},{8,10},{9,11},{10,... | collective-permute-start | bytes 294920 | tf_op jit(solution)/shard_map/ppermute | solution.py:28
  98.4 6.3 %collective-permute-start.22 = (bf16[192,256]{1,0:T(8,128)(2,1)S(1)}, bf16[192,256]{1,0:T(8,128)(2,1)S(1)}, u32[]{:S(2)}, u32[]{:S(2)}) collective-permute-start(bf16[192,256]{1,0:T(8,128)(2,1)S(1)} %get-tuple-element.83), channel_id=1, source_target_pairs={{0,3},{1,0},{2,1},{3,2},{4,7},{5,4},{6,5},{7,6},{8,11},{9,8},{10,9... | collective-permute-start | bytes 294920 | tf_op jit(solution)/shard_map/ppermute | solution.py:28
  105.5 7.6 %collective-permute-start.23 = (bf16[192,256]{1,0:T(8,128)(2,1)S(1)}, bf16[192,256]{1,0:T(8,128)(2,1)S(1)}, u32[]{:S(2)}, u32[]{:S(2)}) collective-permute-start(bf16[192,256]{1,0:T(8,128)(2,1)S(1)} %update.2.x), channel_id=1, source_target_pairs={{0,4},{1,5},{2,6},{3,7},{4,8},{5,9},{6,10},{7,11},{8,12},{9,13},{1... | collective-permute-start | bytes 294920 | tf_op jit(solution)/shard_map/ppermute | solution.py:28
  107.5 8.2 %collective-permute-start.24 = (bf16[192,256]{1,0:T(8,128)(2,1)S(1)}, bf16[192,256]{1,0:T(8,128)(2,1)S(1)}, u32[]{:S(2)}, u32[]{:S(2)}) collective-permute-start(bf16[192,256]{1,0:T(8,128)(2,1)S(1)} %update.2.x), channel_id=1, source_target_pairs={{0,8},{1,9},{2,10},{3,11},{4,12},{5,13},{6,14},{7,15},{8,0},{9,1},... | collective-permute-start | bytes 294920 | tf_op jit(solution)/shard_map/ppermute | solution.py:28
  109.6 6.1 %collective-permute-start.25 = (bf16[192,256]{1,0:T(8,128)(2,1)S(1)}, bf16[192,256]{1,0:T(8,128)(2,1)S(1)}, u32[]{:S(2)}, u32[]{:S(2)}) collective-permute-start(bf16[192,256]{1,0:T(8,128)(2,1)S(1)} %update.2.x), channel_id=1, source_target_pairs={{0,12},{1,13},{2,14},{3,15},{4,0},{5,1},{6,2},{7,3},{8,4},{9,5},{1... | collective-permute-start | bytes 294920 | tf_op jit(solution)/shard_map/ppermute | solution.py:28
  115.8 11.2 %collective-permute-start.26 = (bf16[4,192,256]{2,1,0:T(8,128)(2,1)S(1)}, bf16[4,192,256]{2,1,0:T(8,128)(2,1)S(1)}, u32[]{:S(2)}, u32[]{:S(2)}) collective-permute-start(bf16[4,192,256]{2,1,0:T(8,128)(2,1)S(1)} %pad_maximum_fusion.2.refs_0_), channel_id=1, source_target_pairs={{0,1},{1,2},{2,3},{3,0},{4,5},{5,6},{6,7},{7,4},{8,9},{9,10},{10,1... | collective-permute-start | bytes 1179656 | tf_op jit(solution)/shard_map/ppermute | solution.py:28
  116.2 12.0 %collective-permute-start.27 = (bf16[4,192,256]{2,1,0:T(8,128)(2,1)S(1)}, bf16[4,192,256]{2,1,0:T(8,128)(2,1)S(1)}, u32[]{:S(2)}, u32[]{:S(2)}) collective-permute-start(bf16[4,192,256]{2,1,0:T(8,128)(2,1)S(1)} %pad_maximum_fusion.2.refs_0_), channel_id=1, source_target_pairs={{0,3},{1,0},{2,1},{3,2},{4,7},{5,4},{6,5},{7,6},{8,11},{9,8},{10,9... | collective-permute-start | bytes 1179656 | tf_op jit(solution)/shard_map/ppermute | solution.py:28
  128.6 7.0 %collective-permute-start.29 = (bf16[2,192,256]{2,1,0:T(8,128)(2,1)S(1)}, bf16[2,192,256]{2,1,0:T(8,128)(2,1)S(1)}, u32[]{:S(2)}, u32[]{:S(2)}) collective-permute-start(bf16[2,192,256]{2,1,0:T(8,128)(2,1)S(1)} %slice.15), channel_id=1, source_target_pairs={{0,3},{1,0},{2,1},{3,2},{4,7},{5,4},{6,5},{7,6},{8,11},{9,8},{10,9... | collective-permute-start | bytes 589832 | tf_op jit(solution)/shard_map/ppermute | solution.py:28
  150.3 6.9 %collective-permute-start.30 = (bf16[128,256]{1,0:T(8,128)(2,1)S(1)}, bf16[128,256]{1,0:T(8,128)(2,1)S(1)}, u32[]{:S(2)}, u32[]{:S(2)}) collective-permute-start(bf16[128,256]{1,0:T(8,128)(2,1)S(1)} %attend.3.refs_0_), channel_id=1, source_target_pairs={{0,4},{1,5},{2,6},{3,7},{4,8},{5,9},{6,10},{7,11},{8,12},{9,13},{1... | collective-permute-start | bytes 196616 | tf_op jit(solution)/shard_map/ppermute | solution.py:28
  151.0 8.3 %collective-permute-start.31 = (bf16[128,256]{1,0:T(8,128)(2,1)S(1)}, bf16[128,256]{1,0:T(8,128)(2,1)S(1)}, u32[]{:S(2)}, u32[]{:S(2)}) collective-permute-start(bf16[128,256]{1,0:T(8,128)(2,1)S(1)} %attend.3.refs_0_), channel_id=1, source_target_pairs={{0,8},{1,9},{2,10},{3,11},{4,12},{5,13},{6,14},{7,15},{8,0},{9,1},... | collective-permute-start | bytes 196616 | tf_op jit(solution)/shard_map/ppermute | solution.py:28
  151.0 8.3 %collective-permute-start.32 = (bf16[128,256]{1,0:T(8,128)(2,1)S(1)}, bf16[128,256]{1,0:T(8,128)(2,1)S(1)}, u32[]{:S(2)}, u32[]{:S(2)}) collective-permute-start(bf16[128,256]{1,0:T(8,128)(2,1)S(1)} %attend.3.refs_0_), channel_id=1, source_target_pairs={{0,12},{1,13},{2,14},{3,15},{4,0},{5,1},{6,2},{7,3},{8,4},{9,5},{1... | collective-permute-start | bytes 196616 | tf_op jit(solution)/shard_map/ppermute | solution.py:28
  160.9 6.5 %collective-permute-start.34 = (bf16[192,256]{1,0:T(8,128)(2,1)S(1)}, bf16[192,256]{1,0:T(8,128)(2,1)S(1)}, u32[]{:S(2)}, u32[]{:S(2)}) collective-permute-start(bf16[192,256]{1,0:T(8,128)(2,1)S(1)} %get-tuple-element.95), channel_id=1, source_target_pairs={{0,2},{1,3},{2,0},{3,1},{4,6},{5,7},{6,4},{7,5},{8,10},{9,11},{10,... | collective-permute-start | bytes 294920 | tf_op jit(solution)/shard_map/ppermute | solution.py:28
  (20 other events, 144.0 us)
Sparse Core Ops, SparseCore 0:
  10.7 69.8 all-gather.3
  83.2 62.0 all-gather.5
